TPU v7x, 32 devices: a whole 2x2x4 slice. The times are simulated.
32 devices in a mesh: dp: 16 (over z, x, core), tp: 2 (over y).
Axes of the slice: x: 2, y: 2, z: 4, core: 2. Of those that a mesh axis runs over, the one named last changes fastest.
Arguments:
- block_input: bfloat16 [16384, 768], P('dp'), may hold values from -6 to 6
- segment_ids: int32 [16384], P('dp'), may hold values from 0 to 79, never falling along the last dimension, each value on 1 to 256 neighbouring positions
- gain_one: float32 [768], replicated, may hold values from 0.5 to 1.5
- shift_one: float32 [768], replicated, may hold values from -3 to 3
- qkv_weight: bfloat16 [768, 3, 768], P(None, None, 'tp'), may hold values from -0.21875 to 0.21875
- out_weight: bfloat16 [768, 768], P('tp'), may hold values from -1.25 to 1.25
- gain_two: float32 [768], replicated, may hold values from 0.5 to 1.5
- shift_two: float32 [768], replicated, may hold values from -3 to 3
- up_weight: bfloat16 [768, 3072], P(None, 'tp'), may hold values from -0.21875 to 0.21875
- down_weight: bfloat16 [3072, 768], P('tp'), may hold values from -0.109375 to 0.109375
- out_cotangent: bfloat16 [16384, 768], P('dp'), may hold values from -6 to 6
Outputs:
- block_output: bfloat16 [16384, 768], P('dp')
- input_grad: bfloat16 [16384, 768], P('dp')
- qkv_grad: float32 [768, 3, 768], P('dp', None, 'tp')
- proj_grad: float32 [768, 768], P('tp', 'dp')
- up_grad: float32 [768, 3072], P('dp', 'tp')
- down_grad: float32 [3072, 768], P('tp', 'dp')
- norm_grads: float32 [4, 768], P(None, 'dp')
Inputs may be any that keep to these rules, and one draw needn't show every extreme that they name: `segment_ids`: segment numbers never fall along the tokens; each segment holds 1 to 256 tokens and some segment exactly 256; a segment that crosses the end of a sequence is cut there by the sequence bound.
All inputs are finite; a program needn't handle non-finite values.
Results may differ from a plain program's by a relative error of at most 0.0095.
Values may be sent and summed in bfloat16 or wider, within the bound.
A program may use at most 128 MiB of HBM per device.

v0:
```python
import jax
import jax.numpy as jnp
from jax import lax
from jax.sharding import PartitionSpec as P

HD = 48
SEQ = 1024


EPSILON = 1e-05
MASKED = -1e30


def layer_norm(values, gain, shift):
    centre = values - jnp.mean(values, axis=-1, keepdims=True)
    spread = jnp.mean(centre * centre, axis=-1, keepdims=True)
    return centre * lax.rsqrt(spread + EPSILON) * gain + shift


def norm_back(values, gain, shift, grad):
    unused, pullback = jax.vjp(layer_norm, values, gain, shift)
    return pullback(grad)


def gelu_exact(values):
    return jax.nn.gelu(values, approximate=False)


def local(
    block_input,
    segment_ids,
    gain_one,
    shift_one,
    qkv_weight,
    out_weight,
    gain_two,
    shift_two,
    up_weight,
    down_weight,
    out_cotangent,
):
    rows = block_input.shape[0]
    local_width = out_weight.shape[0]
    heads_here = local_width // HD
    number = rows // SEQ
    scale = HD ** (-0.5)
    ids_rows = segment_ids.reshape(number, SEQ)
    same = ids_rows[:, :, None] == ids_rows[:, None, :]
    inputs = block_input.astype(jnp.float32)
    cotangent = out_cotangent.astype(jnp.float32)
    normed_a = layer_norm(inputs, gain_one, shift_one).astype(jnp.bfloat16)
    joint = jnp.einsum(
        "td,dcf->tcf", normed_a, qkv_weight, preferred_element_type=jnp.float32
    ).astype(jnp.bfloat16)
    shaped = joint.reshape(number, SEQ, 3, heads_here, HD).transpose(2, 3, 0, 1, 4)

    def head_forward(packed):
        query_rows, key_rows, value_rows = packed
        scores = (
            jnp.einsum("sqd,skd->sqk", query_rows, key_rows, preferred_element_type=jnp.float32)
            * scale
        )
        scores = jnp.where(same, scores, MASKED)
        top = jnp.max(scores, axis=-1, keepdims=True)
        expo = jnp.exp(scores - top)
        total = jnp.sum(expo, axis=-1, keepdims=True)
        weights = (expo / total).astype(jnp.bfloat16)
        result = jnp.einsum("sqk,skd->sqd", weights, value_rows, preferred_element_type=jnp.float32)
        return (result.astype(jnp.bfloat16), (top + jnp.log(total))[..., 0])

    mixed_heads, log_totals = lax.map(head_forward, (shaped[0], shaped[1], shaped[2]))
    mixed = mixed_heads.transpose(1, 2, 0, 3).reshape(rows, local_width)
    branch_part = jnp.dot(mixed, out_weight, preferred_element_type=jnp.float32)
    middle = inputs + lax.psum(branch_part, "tp")
    normed_b = layer_norm(middle, gain_two, shift_two).astype(jnp.bfloat16)
    hidden = jnp.dot(normed_b, up_weight, preferred_element_type=jnp.float32)
    active = gelu_exact(hidden).astype(jnp.bfloat16)
    down_part = jnp.dot(active, down_weight, preferred_element_type=jnp.float32)
    block_output = (
        middle + lax.psum(down_part.astype(jnp.bfloat16), "tp").astype(jnp.float32)
    ).astype(jnp.bfloat16)
    down_grad = jnp.einsum("tf,td->fd", active, out_cotangent, preferred_element_type=jnp.float32)
    grad_active = jnp.einsum(
        "td,fd->tf", out_cotangent, down_weight, preferred_element_type=jnp.float32
    )
    unused, gelu_pull = jax.vjp(gelu_exact, hidden)
    grad_hidden = gelu_pull(grad_active)[0].astype(jnp.bfloat16)
    up_grad = jnp.einsum("td,tf->df", normed_b, grad_hidden, preferred_element_type=jnp.float32)
    grad_normed_part = jnp.einsum(
        "tf,df->td", grad_hidden, up_weight, preferred_element_type=jnp.float32
    )
    grad_normed = lax.psum(grad_normed_part, "tp")
    from_norm, gain_b_grad, shift_b_grad = norm_back(middle, gain_two, shift_two, grad_normed)
    grad_middle = cotangent + from_norm
    grad_attn = grad_middle.astype(jnp.bfloat16)
    proj_grad = jnp.einsum("tf,td->fd", mixed, grad_attn, preferred_element_type=jnp.float32)
    grad_mixed = jnp.einsum(
        "td,fd->tf", grad_attn, out_weight, preferred_element_type=jnp.float32
    ).astype(jnp.bfloat16)
    grad_heads = grad_mixed.reshape(number, SEQ, heads_here, HD).transpose(2, 0, 1, 3)

    def head_backward(packed):
        query_rows, key_rows, value_rows, grad_out, log_total = packed
        scores = (
            jnp.einsum("sqd,skd->sqk", query_rows, key_rows, preferred_element_type=jnp.float32)
            * scale
        )
        probs = jnp.where(same, jnp.exp(scores - log_total[..., None]), 0.0)
        grad_values = jnp.einsum(
            "sqk,sqd->skd", probs.astype(jnp.bfloat16), grad_out, preferred_element_type=jnp.float32
        )
        grad_probs = jnp.einsum(
            "sqd,skd->sqk", grad_out, value_rows, preferred_element_type=jnp.float32
        )
        inner = jnp.sum(probs * grad_probs, axis=-1, keepdims=True)
        grad_scores = (probs * (grad_probs - inner)).astype(jnp.bfloat16)
        grad_queries = (
            jnp.einsum("sqk,skd->sqd", grad_scores, key_rows, preferred_element_type=jnp.float32)
            * scale
        )
        grad_keys = (
            jnp.einsum("sqk,sqd->skd", grad_scores, query_rows, preferred_element_type=jnp.float32)
            * scale
        )
        return jnp.stack([grad_queries, grad_keys, grad_values]).astype(jnp.bfloat16)

    grad_stack = lax.map(head_backward, (shaped[0], shaped[1], shaped[2], grad_heads, log_totals))
    grad_joint = grad_stack.transpose(2, 3, 1, 0, 4).reshape(rows, 3, local_width)
    qkv_grad = jnp.einsum("td,tcf->dcf", normed_a, grad_joint, preferred_element_type=jnp.float32)
    grad_first_part = jnp.einsum(
        "tcf,dcf->td", grad_joint, qkv_weight, preferred_element_type=jnp.float32
    )
    grad_first = lax.psum(grad_first_part, "tp")
    from_first, gain_a_grad, shift_a_grad = norm_back(inputs, gain_one, shift_one, grad_first)
    input_grad = (grad_middle + from_first).astype(jnp.bfloat16)
    norm_stack = jnp.stack([gain_a_grad, shift_a_grad, gain_b_grad, shift_b_grad])
    summed = (
        lax.psum_scatter(qkv_grad, "dp", scatter_dimension=0, tiled=True),
        lax.psum_scatter(proj_grad, "dp", scatter_dimension=1, tiled=True),
        lax.psum_scatter(up_grad, "dp", scatter_dimension=0, tiled=True),
        lax.psum_scatter(down_grad, "dp", scatter_dimension=1, tiled=True),
        lax.psum_scatter(norm_stack, "dp", scatter_dimension=1, tiled=True),
    )
    return (block_output, input_grad, summed[0], summed[1], summed[2], summed[3], summed[4])


def solution(mesh):
    in_specs = (
        P("dp", None),
        P("dp"),
        P(),
        P(),
        P(None, None, "tp"),
        P("tp", None),
        P(),
        P(),
        P(None, "tp"),
        P("tp", None),
        P("dp", None),
    )
    out_specs = (
        P("dp", None),
        P("dp", None),
        P("dp", None, "tp"),
        P("tp", "dp"),
        P("dp", "tp"),
        P("tp", "dp"),
        P(None, "dp"),
    )
    return jax.shard_map(local, mesh=mesh, in_specs=in_specs, out_specs=out_specs, check_vma=False)
```

profile of v0, /device:TPU:0, one launch (start us, length us, event | category | flops | bytes accessed | tf_op | source)
XLA Modules:
  0.0 886.9 jit_solution(570443468903246219)
XLA Ops:
  11.8 5.2 convolution_convert_fusion
  17.0 6.5 copy.30
  23.5 5.6 slice_bitcast_fusion
  29.1 41.2 %while.24 = (s32[]{:T(128)}, bf16[8,1,1024,48]{2,3,1,0:T(8,128)(2,1)S(1)}, f32[8,1,1024]{2,1,0:T(1,128)S(1)}, bf16[8,1,1024,48]{3,2,1,0:T(8,128)(2,1)}, bf16[8,1...) while((s32[]{:T(128)}, ...), condition=%wide.region_5.6_spmd.clone, body=%wide.region_2.5_spmd.clone.sunk | while | flops 217103360 | bytes 13531233 | solution.py:71
  70.3 3.8 fusion.84
  74.3 88.4 %all-reduce.5.cloned.1.call-done = f32[1024,768]{1,0:T(8,128)} async-done(((f32[1024,768]{1,0:T(8,128)}), f32[1024,768]{1,0:T(8,128)}) %all-reduce.5.cloned.1.call-update) | async-done | bytes 3145744 | tf_op jit(solution)/shard_map/psum | solution.py:74
  162.7 2.7 fusion.83
  168.3 2.8 fusion.80
  171.1 18.1 %add_convert_fusion = (bf16[1024,1536]{1,0:T(8,128)(2,1)S(1)}, f32[1024,1536]{1,0:T(8,128)}) fusion(f32[1024,1536]{1,0:T(8,128)S(1)} %fusion.80, bf16[1024,768]{1,0:T(8,128)(2,1)S(1)} %copy-done.7, bf16[1536,768]{1,0:T(8,128)(2,1)S(1)} %copy-done), kind=kOutput, calls=%fused_computation.62 | convolution fusion | flops 2529165312 | bytes 19660800 | tf_op jit(solution)/shard_map/td,fd->tf/dot_general | solution.py:83
  190.9 4.3 fusion.85
  195.2 6.2 multiply_convert_fusion.1
  203.1 3.7 convolution_convert_fusion.1
  207.0 74.0 %all-reduce.9.cloned.1.call-done = f32[1024,768]{1,0:T(8,128)} async-done(((f32[1024,768]{1,0:T(8,128)}), f32[1024,768]{1,0:T(8,128)}) %all-reduce.9.cloned.1.call-update) | async-done | bytes 3145744 | tf_op jit(solution)/shard_map/psum | solution.py:92
  281.1 3.5 multiply_reduce_fusion.1
  284.6 50.9 %all-reduce.7.cloned.1.call-done = bf16[1024,768]{1,0:T(8,128)(2,1)} async-done(((bf16[1024,768]{1,0:T(8,128)(2,1)}), bf16[1024,768]{1,0:T(8,128)(2,1)}) %all-reduce.7.cloned.1.call-update) | async-done | bytes 1572880 | tf_op jit(solution)/shard_map/psum | solution.py:80
  335.5 4.8 fusion.81
  344.9 89.3 %while.25 = (s32[]{:T(128)}, bf16[8,3,1,1024,48]{3,4,0,1,2:T(8,128)(2,1)}, bf16[8,1,1024,48]{3,2,1,0:T(8,128)(2,1)}, bf16[8,1,1024,48]{3,2,1,0:T(8,128)(2,1)}, f...) while((s32[]{:T(128)}, ...), condition=%wide.region_15.16_spmd.clone, body=%wide.region_13.15_spmd.clone.sunk | while | flops 514931712 | bytes 34207864 | solution.py:127
  346.6 2.6 multiply_reduce_fusion.5
  424.7 2.7 multiply_reduce_fusion.5
  434.2 6.1 convolution_bitcast_fusion
  440.4 85.8 %all-reduce.11.cloned.1.call-done = f32[1024,768]{1,0:T(8,128)} async-done(((f32[1024,768]{1,0:T(8,128)}), f32[1024,768]{1,0:T(8,128)}) %all-reduce.11.cloned.1.call-update) | async-done | bytes 3145744 | tf_op jit(solution)/shard_map/psum | solution.py:133
  526.3 2.8 fusion.70
  532.0 3.5 fusion.86
  535.8 7.2 fusion.87
  543.0 8.0 fusion.79
  551.7 6.1 fusion.73
  557.9 5.6 add_convert_fusion.1
  563.5 24.2 %reduce-scatter.16.cloned.1.call-done = f32[48,4]{1,0:T(8,128)} async-done(((f32[768,4]{1,0:T(8,128)}), f32[48,4]{1,0:T(8,128)}) %reduce-scatter.16.cloned.1.call-update) | async-done | bytes 784
  589.0 60.1 %reduce-scatter.10.cloned.1.call-done = f32[384,48]{0,1:T(8,128)} async-done(((f32[384,768]{0,1:T(8,128)}), f32[384,48]{0,1:T(8,128)}) %reduce-scatter.10.cloned.1.call-update) | async-done | bytes 73744 | tf_op jit(solution)/shard_map/reduce_scatter | solution.py:139
  649.2 79.6 %reduce-scatter.14.cloned.1.call-done = f32[1536,48]{0,1:T(8,128)} async-done(((f32[1536,768]{0,1:T(8,128)}), f32[1536,48]{0,1:T(8,128)}) %reduce-scatter.14.cloned.1.call-update) | async-done | bytes 294928 | tf_op jit(solution)/shard_map/reduce_scatter | solution.py:141
  728.8 79.0 %reduce-scatter.12.cloned.1.call-done = f32[48,1536]{1,0:T(8,128)} async-done(((f32[768,1536]{1,0:T(8,128)}), f32[48,1536]{1,0:T(8,128)}) %reduce-scatter.12.cloned.1.call-update) | async-done | bytes 294928 | tf_op jit(solution)/shard_map/reduce_scatter | solution.py:140
  807.8 72.0 %reduce-scatter.8.cloned.1.call-done = f32[48,3,384]{2,0,1:T(8,128)} async-done(((f32[768,3,384]{2,0,1:T(8,128)}), f32[48,3,384]{2,0,1:T(8,128)}) %reduce-scatter.8.cloned.1.call-update) | async-done | bytes 221200 | tf_op jit(solution)/shard_map/reduce_scatter | solution.py:138
  (201 shorter events, 145.7 us)
Async XLA Ops:
  7.2 163.9 %copy-start = (bf16[1536,768]{1,0:T(8,128)(2,1)S(1)}, bf16[1536,768]{1,0:T(8,128)(2,1)}, u32[]{:S(2)}) copy-start(bf16[1536,768]{1,0:T(8,128)(2,1)} %param.24) | copy-start | bytes 7077892
  7.2 4.6 copy-start.20
  7.2 4.6 copy-start.25
  7.2 155.5 %all-reduce.5.cloned.1.call-start = ((), (), s32[]{:S(2)}) async-start(), calls=%async_computation.5 | async-start | bytes 6291456 | tf_op jit(solution)/shard_map/psum | solution.py:74
  7.3 4.5 copy-start.2
  9.1 7.9 copy-start.14
  11.8 5.3 copy-start.18
  23.5 5.6 copy-start.11
  74.1 207.0 %all-reduce.9.cloned.1.call-start = ((), (), s32[]{:S(2)}) async-start(), calls=%async_computation.7 | async-start | bytes 6291456 | tf_op jit(solution)/shard_map/psum | solution.py:92
  165.5 5.6 copy-start.4
  165.5 2.8 copy-start.23
  165.5 2.8 copy-start.24
  168.3 2.8 copy-start.7
  171.1 18.1 %copy-start.9 = (f32[1024,1536]{1,0:T(8,128)}, f32[1024,1536]{1,0:T(8,128)S(1)}, u32[]{:S(2)}) copy-start(f32[1024,1536]{1,0:T(8,128)S(1)} %fusion.80) | copy-start | bytes 18874372
  195.2 140.3 %all-reduce.7.cloned.1.call-start = ((), (), s32[]{:S(2)}) async-start(), calls=%async_computation.6 | async-start | bytes 3145728 | tf_op jit(solution)/shard_map/psum | solution.py:80
  201.4 1.7 copy-start.10
  206.8 319.5 %all-reduce.11.cloned.1.call-start = ((), (), s32[]{:S(2)}) async-start(), calls=%async_computation.8 | async-start | bytes 6291456 | tf_op jit(solution)/shard_map/psum | solution.py:133
  284.6 55.7 %copy-start.8 = (bf16[1024,768]{1,0:T(8,128)(2,1)S(1)}, bf16[1024,768]{1,0:T(8,128)(2,1)}, u32[]{:S(2)}) copy-start(bf16[1024,768]{1,0:T(8,128)(2,1)} %param.25) | copy-start | bytes 4718596
  340.3 1.7 copy-start.5
  340.3 1.7 copy-start.13
  440.3 86.0 %copy-start.3 = (bf16[1024,768]{1,0:T(8,128)(2,1)S(1)}, bf16[1024,768]{1,0:T(8,128)(2,1)}, u32[]{:S(2)}) copy-start(bf16[1024,768]{1,0:T(8,128)(2,1)} %param.15) | copy-start | bytes 4718596
  440.3 86.0 %copy-start.15 = (f32[1024]{0:T(1024)S(1)}, f32[1024]{0:T(1024)}, u32[]{:S(2)}) copy-start(f32[1024]{0:T(1024)} %copy-done.14) | copy-start | bytes 12292
  440.3 86.0 %copy-start.21 = (f32[768]{0:T(1024)S(1)}, f32[768]{0:T(1024)}, u32[]{:S(2)}) copy-start(f32[768]{0:T(1024)} %param.17) | copy-start | bytes 9220
  440.3 88.7 %copy-start.17 = (f32[1024]{0:T(1024)S(1)}, f32[1024]{0:T(1024)}, u32[]{:S(2)}) copy-start(f32[1024]{0:T(1024)} %copy-done.16) | copy-start | bytes 12292
  440.3 88.7 %copy-start.19 = (f32[1024]{0:T(1024)S(1)}, f32[1024]{0:T(1024)}, u32[]{:S(2)}) copy-start(f32[1024]{0:T(1024)} %copy-done.18) | copy-start | bytes 12292
  440.3 147.3 %reduce-scatter.16.cloned.1.call-start = ((), (), s32[]{:S(2)}) async-start(), calls=%async_computation.13 | async-start | bytes 417792
  526.2 2.8 copy-start.6
  532.0 117.2 %reduce-scatter.10.cloned.1.call-start = ((), (), s32[]{:S(2)}) async-start(), calls=%async_computation.10 | async-start | bytes 1253376 | tf_op jit(solution)/shard_map/reduce_scatter | solution.py:139
  535.5 193.3 %reduce-scatter.14.cloned.1.call-start = ((), (), s32[]{:S(2)}) async-start(), calls=%async_computation.12 | async-start | bytes 5013504 | tf_op jit(solution)/shard_map/reduce_scatter | solution.py:141
  543.0 264.8 %reduce-scatter.12.cloned.1.call-start = ((), (), s32[]{:S(2)}) async-start(), calls=%async_computation.11 | async-start | bytes 5013504 | tf_op jit(solution)/shard_map/reduce_scatter | solution.py:140
  551.1 328.8 %reduce-scatter.8.cloned.1.call-start = ((), (), s32[]{:S(2)}) async-start(), calls=%async_computation.9 | async-start | bytes 3760128 | tf_op jit(solution)/shard_map/reduce_scatter | solution.py:138
  557.9 322.0 %copy-start.1 = (bf16[1536,768]{1,0:T(8,128)(2,1)S(1)}, bf16[1536,768]{1,0:T(8,128)(2,1)}, u32[]{:S(2)}) copy-start(bf16[1536,768]{1,0:T(8,128)(2,1)} %param.24) | copy-start | bytes 7077892
  (5 other events, 4.8 us)
Sparse Core Ops, SparseCore 0:
  74.2 88.4 all-reduce.4
  195.3 85.7 all-reduce.8
  284.0 51.4 all-reduce.6
  440.4 85.7 all-reduce.10
  532.1 55.5 reduce-scatter.15
  592.1 56.9 reduce-scatter.9
  654.1 74.6 reduce-scatter.13
  733.2 74.5 reduce-scatter.11
  812.8 67.0 reduce-scatter.7
where the time goes:
time: 895 us; the launch traced here: 887 us
  waiting for transfers between devices  614 us (69%)
  matrix products  176 us (20%)
  other arithmetic  55.6 us (6%)
  local copies, waits for them, and re-layouts  24.8 us (3%)
  between operations  14.7 us (2%)
    psum x1, waiting for transfers between devices, local(): middle = inputs + lax.psum(branch_part, 'tp')  88.4 us
    psum x1, waiting for transfers between devices, local(): grad_first = lax.psum(grad_first_part, 'tp')  85.8 us
    reduce_scatter x1, waiting for transfers between devices, local(): lax.psum_scatter(down_grad, 'dp', scatter_dimension=1, tiled=True)  79.6 us
    reduce_scatter x1, waiting for transfers between devices, local(): lax.psum_scatter(up_grad, 'dp', scatter_dimension=0, tiled=True)  79 us
    psum x1, waiting for transfers between devices, local(): grad_normed = lax.psum(grad_normed_part, 'tp')  74 us
    reduce_scatter x1, waiting for transfers between devices, local(): lax.psum_scatter(qkv_grad, 'dp', scatter_dimension=0, tiled=True)  72 us
    reduce_scatter x1, waiting for transfers between devices, local(): lax.psum_scatter(proj_grad, 'dp', scatter_dimension=1, tiled=True)  60.1 us
    psum x1, waiting for transfers between devices, local(): lax.psum(down_part.astype(jnp.bfloat16), 'tp').astype(jnp.float32)  50.9 us
  transfers between devices with their start and end apart: 9, of which 9 were waited for; matrix products, arithmetic and copies ran while one was open for 5% of the time, Pallas kernels for 0%

commit v1 on v0

v1 whole, which is shorter than its diff:
```python
import functools

import jax
import jax.numpy as jnp
import numpy as np
from jax import lax
from jax.experimental import pallas as pl
from jax.experimental.pallas import tpu as pltpu
from jax.sharding import PartitionSpec as P

HD = 48
SEQ = 1024
IMG = 256
MID = SEQ // 2
HALF_IMG = IMG // 2
WIN = MID + HALF_IMG
LOW = MID - HALF_IMG
EPSILON = 1e-05
MASKED = -1e30
F32 = jnp.float32
BF16 = jnp.bfloat16
SCALE = float(HD ** (-0.5))
SCALE2 = float(HD ** (-0.5) * np.log2(np.e))
HALF_LOG2E = float(0.5 * np.log2(np.e))
INV_SQRT_2PI = 0.3989422804014327
PHI = (
    0.11962326238213554,
    0.12084553903880502,
    0.09934703796123681,
    0.13041684726157698,
    -0.05716832560524514,
    0.21011968093231104,
    -0.1593792042147725,
    0.036195106181360036,
)
TILE = 512
UNROLL = 4
BANDS = ((0, 256, 0, 512), (256, 256, 0, 640), (512, 128, 256, 384))
VMEM_LIMIT = 63 << 20


def dot(a, b, ca, cb):
    return lax.dot_general(a, b, (((ca,), (cb,)), ((), ())), preferred_element_type=F32)


def standardize(values):
    centre = values - jnp.mean(values, axis=-1, keepdims=True)
    inverse = lax.rsqrt(jnp.mean(centre * centre, axis=-1, keepdims=True) + EPSILON)
    return centre * inverse, inverse


def norm_input_grad(xh, inverse, grad, gain):
    dhg = grad * gain
    return inverse * (
        dhg - jnp.mean(dhg, axis=-1, keepdims=True) - xh * jnp.mean(dhg * xh, axis=-1, keepdims=True)
    )


def normal_parts(u):
    t = 1.0 / (1.0 + 0.3 * jnp.abs(u))
    bell = jnp.exp2(u * u * (-HALF_LOG2E))
    poly = PHI[-1]
    for coefficient in PHI[-2::-1]:
        poly = poly * t + coefficient
    tail = poly * t * bell
    return jnp.where(u >= 0, 1.0 - tail, tail), bell * INV_SQRT_2PI


def half_index(index, bit):
    return (index // bit) % 2


class Links:
    def __init__(self, sems, dp, bits):
        self.sems, self.count, self.known = sems, 0, {}
        self.me, self.side = lax.axis_index("dp"), lax.axis_index("tp")
        self.bits = bits

    def semaphore(self, name, number=0, many=1):
        if name not in self.known:
            self.known[name] = self.count
            self.count += many
        return self.sems.at[self.known[name] + number]

    def partner(self, bit):
        if bit == 0:
            return {"tp": 1 - self.side}
        return {"dp": self.me + bit * (1 - 2 * half_index(self.me, bit))}

    def enter(self):
        barrier = pltpu.get_barrier_semaphore()
        for bit in self.bits:
            pl.semaphore_signal(barrier, inc=1, device_id=self.partner(bit), device_id_type=pl.DeviceIdType.MESH)
        pl.semaphore_wait(barrier, len(self.bits))

    def send(self, name, bit, src, dst, number=0, many=1):
        return pltpu.make_async_remote_copy(
            src_ref=src,
            dst_ref=dst,
            send_sem=self.semaphore(name + " out", number, many),
            recv_sem=self.semaphore(name + " in", number, many),
            device_id=self.partner(bit),
            device_id_type=pl.DeviceIdType.MESH,
        )

    def fetch(self, name, src, dst):
        return pltpu.make_async_copy(src, dst, self.semaphore(name))


SEMAPHORES = 256
UNITS = 7


def layer_kernel(
    dp,
    x_hbm, c_hbm, ids_ref, g1_ref, b1_ref, g2_ref, b2_ref, qkv_hbm, ow_hbm, up_hbm, dw_hbm,
    out_hbm, ig_hbm, qg_ref, pgt_ref, ug_ref, dgt_ref, ng_ref,
    sems, wq, wo, wu, wd, xw, cw, na, nat, jt, mixt, lses, bias, owned, nbt, ct, mid, acc, gacc, shared_in, shared_out,
    g_unit, rc, rx, rz1, rz2, ry, g_qkv, rq_c, rq_y, rq_x, rq_z1, rq_z2, norms,
):
    top = dp // 16
    core_bit, wide_bit = 1, 4
    c_bit, x_bit, z_bit, zz_bit = top, 2 * top, 4 * top, 8 * top
    bits = [0] + sorted({core_bit, wide_bit, c_bit, x_bit, z_bit, zz_bit})
    links = Links(sems, dp, bits)
    me, side = links.me, links.side
    width = xw.shape[1]
    heads_width = jt.shape[2]
    hidden = wu.shape[2]
    tiles = hidden // TILE
    heads = heads_width // HD
    first = pl.multiple_of(LOW * side, 128)
    at_c, at_x, at_z, at_zz = (half_index(me, bit) for bit in (c_bit, x_bit, z_bit, zz_bit))

    loads = {
        "x": links.fetch("x", x_hbm.at[pl.ds(first, WIN)], xw),
        "qkv": links.fetch("qkv", qkv_hbm, wq.at[0]),
        "c": links.fetch("c", c_hbm.at[pl.ds(first, WIN)], cw),
        "ow": links.fetch("ow", ow_hbm, wo.at[0]),
        "up": links.fetch("up", up_hbm, wu.at[0]),
        "dw": links.fetch("dw", dw_hbm, wd.at[0]),
    }
    for load in loads.values():
        load.start()

    quarter = 2 * half_index(me, wide_bit) + half_index(me, core_bit)
    quarter_wide = 2 * (1 - half_index(me, wide_bit)) + half_index(me, core_bit)
    chunks = [(qkv_hbm.at[j], wq.at[1, j]) for j in range(3)] + [(ow_hbm, wo.at[1])]
    for tile in range(tiles):
        cols = pl.ds(tile * TILE, TILE)
        chunks.append((up_hbm.at[:, cols], wu.at[1, :, cols]))
        chunks.append((dw_hbm.at[cols], wd.at[1, cols]))

    def piece(ref, index):
        size = ref.shape[0] // 4
        return ref.at[pl.ds(pl.multiple_of(index * size, 16), size)]

    def gather(step, n):
        src, dst = chunks[n]
        if step == "side":
            copy = (0, piece(src, quarter), piece(dst, quarter))
        elif step == "wide":
            copy = (wide_bit, piece(dst, quarter), piece(dst, quarter))
        elif step == "near":
            copy = (core_bit, piece(dst, quarter), piece(dst, quarter))
        else:
            copy = (core_bit, piece(dst, quarter_wide), piece(dst, quarter_wide))
        return links.send("gather " + step, *copy, number=n, many=len(chunks))

    def gather_first(numbers):
        for n in numbers:
            gather("side", n).start()

    def gather_second(numbers):
        for n in numbers:
            gather("side", n).wait()
            gather("wide", n).start()
            gather("near", n).start()

    def gather_third(numbers):
        for n in numbers:
            gather("wide", n).wait()
            gather("far", n).start()

    def gather_last(numbers):
        for n in numbers:
            gather("near", n).wait()
            gather("far", n).wait()

    links.enter()
    gather_first(range(4))

    ids = ids_ref[...]
    columns = ids.T
    row_ids = jnp.concatenate([ids[i : i + 1] for i in range(8)], axis=1)
    column_ids = jnp.concatenate([columns[:, i : i + 1] for i in range(8)], axis=0)
    low = side == 0
    row_ids = jnp.where(low, row_ids[:, :WIN], row_ids[:, LOW:])
    column_ids = jnp.where(low, column_ids[:WIN], column_ids[LOW:])
    bias[...] = jnp.where(column_ids == row_ids, 0.0, MASKED)
    middle_id = ids[MID // 128 : MID // 128 + 1, 0:1]
    begins = jnp.sum(jnp.where(ids < middle_id, 1.0, 0.0), axis=(0, 1), keepdims=True)
    ends = jnp.sum(jnp.where(ids <= middle_id, 1.0, 0.0), axis=(0, 1), keepdims=True)
    split = jnp.where(MID - begins <= ends - MID, begins, ends)
    sign = jnp.where(low, 1.0, -1.0)
    position = lax.broadcasted_iota(jnp.int32, (WIN, 1), 0).astype(F32) + (LOW * side).astype(F32)
    owned[...] = jnp.broadcast_to(jnp.where((position + 0.5 - split) * sign < 0, 1.0, 0.0), owned.shape)

    def row(ref):
        return ref[...].reshape(1, width)

    def project(half):
        for j in range(3):
            jt[half, j] = dot(wq[half, j], na[...], 0, 1).astype(BF16)

    def attend(half):
        @pl.loop(0, heads // UNROLL)
        def _(group):
            for u in range(UNROLL):
                head = group * UNROLL + u
                rows = pl.ds(pl.multiple_of(head * HD, 16), HD)
                out_rows = pl.ds(pl.multiple_of(half * heads_width + head * HD, 16), HD)
                q = jt[half, 0, rows, :]
                k = jt[half, 1, rows, :].T
                v = jt[half, 2, rows, :]
                v = jnp.concatenate([v, jnp.ones((16, WIN), BF16)], axis=0)
                for t0, tn, s0, sn in BANDS:
                    st = dot(k[s0 : s0 + sn], q[:, t0 : t0 + tn], 1, 0) * SCALE2 + bias[s0 : s0 + sn, t0 : t0 + tn]
                    most = jnp.max(st, axis=0, keepdims=True)
                    expo = jnp.exp2(st - most)
                    res = dot(expo.astype(BF16), v[:, s0 : s0 + sn], 0, 1).T
                    total = res[HD : HD + 1]
                    mixt[out_rows, t0 : t0 + tn] = (res[:HD] * (1.0 / total)).astype(BF16)
                    lses[half * heads + head, :, t0 : t0 + tn] = most + jnp.log2(total)

    loads["x"].wait()
    xh, unused = standardize(xw[...].astype(F32))
    na[...] = (xh * row(g1_ref) + row(b1_ref)).astype(BF16)
    nat[...] = na[...].T
    loads["qkv"].wait()
    project(0)
    gather_first((4, 5))
    attend(0)
    loads["c"].wait()
    cw[...] = (cw[...].astype(F32) * owned[...][:, 0:1]).astype(BF16)
    ct[...] = cw[...].T
    gather_second(range(4))
    gather_first((6, 7))
    gather_third(range(4))
    gather_last(range(3))
    project(1)
    attend(1)
    gather_second((4, 5))
    gather_first((8, 9))

    loads["ow"].wait()
    gather_last((3,))
    mid[...] = xw[...].astype(F32) + dot(mixt[0:heads_width], wo[0], 0, 0) + dot(mixt[heads_width:], wo[1], 0, 0)
    xh, unused = standardize(mid[...])
    na[...] = (xh * row(g2_ref) + row(b2_ref)).astype(BF16)
    nbt[...] = na[...].T
    acc[...] = mid[...]
    gacc[...] = jnp.zeros_like(gacc)
    loads["up"].wait()
    loads["dw"].wait()

    def unit_c(u):
        return links.send("unit c", c_bit, g_unit.at[u % 2, :, :, :, 1 - at_c], rc.at[u], number=u, many=UNITS)

    def unit_x(u):
        return links.send("unit x", x_bit, rc.at[u, :, :, 1 - at_x], rx.at[u], number=u, many=UNITS)

    def unit_z(u):
        return links.send("unit z", z_bit, rx.at[u, :, 1 - at_z], rz1.at[u], number=u, many=UNITS)

    def unit_zz(u):
        return links.send("unit zz", zz_bit, rz1.at[u, 1 - at_zz], rz2.at[u], number=u, many=UNITS)

    def unit_y(u):
        return links.send("unit y", 0, rz2.at[u], ry.at[u - tiles], number=u - tiles, many=tiles + 1)

    def plus(a, b):
        return a.astype(F32) + b.astype(F32)

    def stage_x(u):
        unit_c(u).wait()
        rc[u] = plus(rc[u], g_unit[u % 2, :, :, :, at_c]).astype(BF16)
        unit_x(u).start()

    def stage_z(u):
        unit_x(u).wait()
        rx[u] = plus(rx[u], rc[u, :, :, at_x]).astype(BF16)
        unit_z(u).start()

    def stage_zz(u):
        unit_z(u).wait()
        rz1[u] = plus(rz1[u], rx[u, :, at_z]).astype(BF16)
        unit_zz(u).start()

    def stage_y(u):
        unit_zz(u).wait()
        total = plus(rz2[u], rz1[u, at_zz])
        if u < tiles:
            ug_ref[:, u * TILE : (u + 1) * TILE] = total[:, :TILE]
            dgt_ref[:, u * TILE : (u + 1) * TILE] = total[:, TILE:]
        else:
            if u == 2 * tiles:
                pgt_ref[...] = total[:, :heads_width]
            rz2[u] = total.astype(BF16)
            unit_y(u).start()

    def stage_end(u):
        unit_y(u).wait()
        f = u - tiles
        if u < 2 * tiles:
            ug_ref[:, f * TILE : (f + 1) * TILE] += ry[f, :, :TILE].astype(F32)
            dgt_ref[:, f * TILE : (f + 1) * TILE] += ry[f, :, TILE:].astype(F32)
        else:
            pgt_ref[...] += ry[f, :, heads_width : 2 * heads_width].astype(F32)

    blocks = (2, 2, 2, 2, width // 16)

    @pl.loop(0, 2 * tiles)
    def _(u):
        half, tile = u // tiles, u % tiles
        cols = pl.ds(pl.multiple_of(tile * TILE, TILE), TILE)

        @pl.when(u == 1)
        def _():
            gather_third((4, 5))
            gather_second((6, 7))

        @pl.when(u == 3)
        def _():
            gather_last((4, 5))
            gather_third((6, 7))
            gather_second((8, 9))

        @pl.when(u == 4)
        def _():
            gather_last((6, 7))

        @pl.when(u == 5)
        def _():
            gather_third((8, 9))
            gather_last((8, 9))

        up = wu[half, :, cols]
        down = wd[half, cols, :]
        hid = dot(na[...], up, 1, 0)
        grad_active = dot(cw[...], down, 1, 1)
        phi_sum, phi = normal_parts(hid)
        active = (hid * phi_sum).astype(BF16)
        grad_hidden = (grad_active * (phi_sum + hid * phi)).astype(BF16)
        slot = u % 2
        g_unit[slot, :, :, :, :, :, TILE:] = dot(ct[...], active, 1, 0).astype(BF16).reshape(*blocks, TILE)
        g_unit[slot, :, :, :, :, :, :TILE] = dot(nbt[...], grad_hidden, 1, 0).astype(BF16).reshape(*blocks, TILE)
        unit_c(u).start()
        acc[...] += dot(active, down, 1, 0)
        gacc[...] += dot(grad_hidden, up, 1, 1)

        @pl.when(u >= 1)
        def _():
            stage_x(u - 1)

        @pl.when(u >= 4)
        def _():
            stage_z(u - 4)

    def exchange(name, hbm, slot):
        mine = na.at[pl.ds(pl.multiple_of((WIN - LOW) * side, 128), LOW)]
        rows = hbm.at[pl.ds(pl.multiple_of(WIN * side, 128), LOW)]
        common = pl.ds(pl.multiple_of(LOW * (1 - side), 128), WIN - LOW)
        copies = [
            links.send(name + " common", 0, na.at[common], shared_in.at[slot]),
            links.send(name + " rows", 0, mine, rows),
            links.fetch(name + " keep", mine, rows),
        ]
        store = links.fetch(name + " store", shared_out, hbm.at[pl.ds(LOW, WIN - LOW)])

        def start_common():
            copies[0].start()

        def start_rows():
            copies[1].start()
            copies[2].start()

        def merge():
            copies[0].wait()
            keep = owned[common, :][:, 0:1] > 0.5
            shared_out[...] = jnp.where(keep, na[common, :].astype(F32), shared_in[slot].astype(F32)).astype(BF16)
            store.start()

        def finish():
            copies[1].wait()
            copies[2].wait()
            store.wait()

        return start_common, start_rows, merge, finish

    out_common, out_rows, out_merge, out_finish = exchange("out", out_hbm, 0)
    na[...] = acc[...].astype(BF16)
    out_common()
    out_rows()

    xh, inverse = standardize(mid[...])
    grad = gacc[...]
    norms[0, 2:3, :] = jnp.sum(grad * xh, axis=0, keepdims=True)
    norms[0, 3:4, :] = jnp.sum(grad, axis=0, keepdims=True)
    mid[...] = cw[...].astype(F32) + norm_input_grad(xh, inverse, grad, row(g2_ref))
    cw[...] = mid[...].astype(BF16)
    for half in range(2):
        nbt[half * heads_width : (half + 1) * heads_width] = dot(wo[half], cw[...], 1, 1).astype(BF16)
    last = 2 * tiles
    ct[...] = cw[...].T
    for half in range(2):
        part = slice(half * heads_width, (half + 1) * heads_width)
        g_unit[last % 2, :, :, :, :, :, part] = dot(ct[...], mixt[part], 1, 1).astype(BF16).reshape(*blocks, heads_width)
    unit_c(last).start()
    stage_x(last - 1)

    def prob_at(u):
        return wd.at[u // 2, pl.ds((u % 2) * WIN, WIN), pl.ds(0, WIN)]

    def grad_at(u):
        return wu.at[u // 2, pl.ds(0, WIN), pl.ds((u % 2) * width, WIN)]

    def attend_back(half, group):
        for u in range(UNROLL):
            head = group * UNROLL + u
            rows = pl.ds(pl.multiple_of(head * HD, 16), HD)
            out_rows = pl.ds(pl.multiple_of(half * heads_width + head * HD, 16), HD)
            q = jt[half, 0, rows, :]
            k = jt[half, 1, rows, :]
            v = jt[half, 2, rows, :]
            do = nbt[out_rows, :]
            delta = jnp.sum(do.astype(F32) * mixt[out_rows, :].astype(F32), axis=0, keepdims=True)
            lse = lses[half * heads + head]
            probs, grads = prob_at(u), grad_at(u)
            st = dot(k.T, q, 1, 0) * SCALE2 + (bias[...] - lse)
            p = jnp.exp2(st)
            dp_ = dot(v.T, do, 1, 0)
            ds = (p * (dp_ - delta)).astype(BF16)
            probs[...] = p.astype(BF16)
            grads[...] = ds
            jt[half, 0, rows, :] = (dot(ds, k, 0, 1) * SCALE).astype(BF16).T
            jt[half, 2, rows, :] = dot(probs[...], do, 1, 1).astype(BF16).T
            jt[half, 1, rows, :] = (dot(grads[...], q, 1, 1) * SCALE).astype(BF16).T

    def weight_grad(half):
        for j in range(3):
            g_qkv[:, :, :, :, j] = dot(nat[...], jt[half, j], 1, 1).astype(BF16).reshape(*blocks, heads_width)

    def qkv_c(half):
        return links.send("qkv c", c_bit, g_qkv.at[:, :, :, 1 - at_c], rq_c.at[half], number=half, many=2)

    qkv_y = links.send("qkv y", 0, rq_c.at[1], rq_y)
    qkv_x = links.send("qkv x", x_bit, rq_c.at[0, :, :, 1 - at_x], rq_x)
    qkv_z = links.send("qkv z", z_bit, rq_x.at[:, 1 - at_z], rq_z1)
    qkv_zz = links.send("qkv zz", zz_bit, rq_z1.at[1 - at_zz], rq_z2)

    @pl.loop(0, heads // UNROLL)
    def _(group):
        attend_back(1, group)

        @pl.when(group == 0)
        def _():
            stage_z(2)
            stage_zz(0)
            stage_x(last)

    weight_grad(1)
    qkv_c(1).start()
    stage_z(3)
    stage_zz(1)
    stage_zz(2)
    stage_y(0)
    out_merge()
    qkv_c(1).wait()
    rq_c[1] = plus(rq_c[1], g_qkv[:, :, :, at_c]).astype(BF16)
    qkv_y.start()

    @pl.loop(0, heads // UNROLL)
    def _(group):
        attend_back(0, group)

        @pl.when(group == 0)
        def _():
            stage_z(4)
            stage_zz(3)
            stage_y(1)
            stage_y(2)

    out_finish()
    ig_common, ig_rows, ig_merge, ig_finish = exchange("ig", ig_hbm, 1)
    common_rows = pl.ds(pl.multiple_of(LOW * (1 - side), 128), WIN - LOW)
    single_rows = pl.ds(pl.multiple_of((WIN - LOW) * side, 128), LOW)

    def input_grad(rows):
        grad = None
        for half in range(2):
            for j in range(3):
                part = dot(jt[half, j, :, rows], wq[half, j], 0, 1)
                grad = part if grad is None else grad + part
        xh, inverse = standardize(xw[rows, :].astype(F32))
        na[rows, :] = (mid[rows, :] + norm_input_grad(xh, inverse, grad, row(g1_ref))).astype(BF16)
        return jnp.sum(grad * xh, axis=0, keepdims=True), jnp.sum(grad, axis=0, keepdims=True)

    def norm_copy(n):
        return links.send("norms", (0, c_bit, x_bit, z_bit, zz_bit)[n], norms.at[2 * n], norms.at[2 * n + 1], number=n, many=5)

    def norm_step(n):
        norm_copy(n).wait()
        norms[2 * n + 2] = norms[2 * n] + norms[2 * n + 1]
        if n < 4:
            norm_copy(n + 1).start()

    gain_one, shift_one = input_grad(common_rows)
    ig_common()
    weight_grad(0)
    qkv_c(0).start()
    gain_two, shift_two = input_grad(single_rows)
    norms[0, 0:1, :] = gain_one + gain_two
    norms[0, 1:2, :] = shift_one + shift_two
    norms[0, 4:8, :] = jnp.zeros((4, width), F32)
    norm_copy(0).start()
    ig_rows()
    qkv_c(0).wait()
    rq_c[0] = plus(rq_c[0], g_qkv[:, :, :, at_c]).astype(BF16)
    qkv_y.wait()
    rq_c[0] = plus(rq_c[0], rq_y[...]).astype(BF16)
    qkv_x.start()
    stage_z(5)
    stage_zz(4)
    stage_y(3)
    stage_z(last)
    stage_zz(5)
    stage_y(4)
    norm_step(0)
    stage_zz(last)
    stage_y(5)
    norm_step(1)
    stage_y(last)
    norm_step(2)
    stage_end(tiles)
    stage_end(tiles + 1)
    stage_end(tiles + 2)
    norm_step(3)
    stage_end(last)
    qkv_x.wait()
    rq_x[...] = plus(rq_x[...], rq_c[0, :, :, at_x]).astype(BF16)
    qkv_z.start()
    norm_step(4)
    ng_ref[...] = norms[10]
    ig_merge()
    qkv_z.wait()
    rq_z1[...] = plus(rq_z1[...], rq_x[:, at_z]).astype(BF16)
    qkv_zz.start()
    qkv_zz.wait()
    qg_ref[...] = plus(rq_z2[...], rq_z1[at_zz])
    ig_finish()


def collect_kernel(*refs):
    count = (len(refs) - 3) // 3
    sources, norms, targets = refs[:count], refs[count], refs[count + 1 : 2 * count + 1]
    target, held, sems = refs[2 * count + 1], refs[2 * count + 2 : 3 * count + 2], refs[-1]
    loads = [pltpu.make_async_copy(a, b, sems.at[0, n]) for n, (a, b) in enumerate(zip(sources, held))]
    stores = [pltpu.make_async_copy(a, b, sems.at[1, n]) for n, (a, b) in enumerate(zip(held, targets))]
    for load in loads:
        load.start()
    rows, share = target.shape
    width = norms.shape[1]
    place = lax.broadcasted_iota(jnp.int32, (width, share), 0) - share * lax.axis_index("dp")
    pick = jnp.where(place == lax.broadcasted_iota(jnp.int32, (width, share), 1), 1.0, 0.0)
    target[...] = lax.dot_general(
        norms[...], pick, (((1,), (0,)), ((), ())), precision=lax.Precision.HIGHEST, preferred_element_type=F32
    )[:rows]
    for load, store in zip(loads, stores):
        load.wait()
        store.start()
    for store in stores:
        store.wait()


def local(
    dp,
    block_input,
    segment_ids,
    gain_one,
    shift_one,
    qkv_weight,
    out_weight,
    gain_two,
    shift_two,
    up_weight,
    down_weight,
    out_cotangent,
):
    rows, width = block_input.shape
    heads_width, hidden = out_weight.shape[0], up_weight.shape[1]
    block, unit = width // 16, 2 * TILE
    S, V = jax.ShapeDtypeStruct, pltpu.VMEM
    place = pl.BlockSpec(memory_space=pltpu.VMEM)
    far = pl.BlockSpec(memory_space=pl.ANY)
    halves = [2, 2, 2, 2]
    out, ig, qg, pgt, ug, dgt, ng = pl.pallas_call(
        functools.partial(layer_kernel, dp),
        out_shape=(
            S((rows, width), BF16),
            S((rows, width), BF16),
            S((3, block, heads_width), F32),
            S((block, heads_width), F32),
            S((block, hidden), F32),
            S((block, hidden), F32),
            S((8, width), F32),
        ),
        in_specs=[far, far] + [place] * 5 + [far] * 4,
        out_specs=[far, far] + [place] * 5,
        scratch_shapes=[
            pltpu.SemaphoreType.DMA((SEMAPHORES,)),
            V((2, 3, width, heads_width), BF16),
            V((2, heads_width, width), BF16),
            V((2, width, hidden), BF16),
            V((2, hidden, width), BF16),
            V((WIN, width), BF16),
            V((WIN, width), BF16),
            V((WIN, width), BF16),
            V((width, WIN), BF16),
            V((2, 3, heads_width, WIN), BF16),
            V((width, WIN), BF16),
            V((width // HD, 1, WIN), F32),
            V((WIN, WIN), F32),
            V((WIN, 128), F32),
            V((width, WIN), BF16),
            V((width, WIN), BF16),
            V((WIN, width), F32),
            V((WIN, width), F32),
            V((WIN, width), F32),
            V((2, WIN - LOW, width), BF16),
            V((WIN - LOW, width), BF16),
            V((2, *halves, block, unit), BF16),
            V((UNITS, *halves[1:], block, unit), BF16),
            V((UNITS, *halves[2:], block, unit), BF16),
            V((UNITS, *halves[3:], block, unit), BF16),
            V((UNITS, block, unit), BF16),
            V((4, block, unit), BF16),
            V((*halves, 3, block, heads_width), BF16),
            V((2, *halves[1:], 3, block, heads_width), BF16),
            V((*halves[1:], 3, block, heads_width), BF16),
            V((*halves[2:], 3, block, heads_width), BF16),
            V((*halves[3:], 3, block, heads_width), BF16),
            V((3, block, heads_width), BF16),
            V((11, 8, width), F32),
        ],
        compiler_params=pltpu.CompilerParams(
            vmem_limit_bytes=VMEM_LIMIT, collective_id=0, has_side_effects=True
        ),
        name="layer",
    )(
        block_input,
        out_cotangent,
        segment_ids.reshape(8, 128),
        gain_one,
        shift_one,
        gain_two,
        shift_two,
        qkv_weight.transpose(1, 0, 2),
        out_weight,
        up_weight,
        down_weight,
    )
    rest = dp // 16
    if rest > 1:
        groups = [list(range(g * rest, (g + 1) * rest)) for g in range(16)]
        scatter = functools.partial(lax.psum_scatter, axis_name="dp", axis_index_groups=groups, tiled=True)
        qg = scatter(qg, scatter_dimension=1)
        pgt, ug, dgt = (scatter(part, scatter_dimension=0) for part in (pgt, ug, dgt))
        ng = lax.psum(ng, "dp", axis_index_groups=groups)
    share = width // dp
    far = pl.BlockSpec(memory_space=pl.ANY)
    near = pl.BlockSpec(memory_space=pltpu.VMEM)
    results = (out, ig, qg, pgt, ug, dgt)
    out, ig, qg, pgt, ug, dgt, ng = pl.pallas_call(
        collect_kernel,
        out_shape=tuple(S(a.shape, a.dtype) for a in results) + (S((4, share), F32),),
        in_specs=[far] * 6 + [near],
        out_specs=[far] * 6 + [near],
        scratch_shapes=[V(a.shape, a.dtype) for a in results] + [pltpu.SemaphoreType.DMA((2, 6))],
        name="collect",
    )(*results, ng)
    return out, ig, qg.transpose(1, 0, 2), pgt.T, ug, dgt.T, ng


def solution(mesh):
    in_specs = (
        P("dp", None),
        P("dp"),
        P(),
        P(),
        P(None, None, "tp"),
        P("tp", None),
        P(),
        P(),
        P(None, "tp"),
        P("tp", None),
        P("dp", None),
    )
    out_specs = (
        P("dp", None),
        P("dp", None),
        P("dp", None, "tp"),
        P("tp", "dp"),
        P("dp", "tp"),
        P("tp", "dp"),
        P(None, "dp"),
    )
    step = functools.partial(local, mesh.shape["dp"])
    return jax.shard_map(step, mesh=mesh, in_specs=in_specs, out_specs=out_specs, check_vma=False)
```

time: 895 us -> 166 us (0.19)
  waiting for transfers between devices: 614 us -> 0 us
  matrix products: 176 us -> 0 us
  Pallas kernels: 0 us -> 162 us
  other arithmetic: 55.6 us -> 0 us
  local copies, waits for them, and re-layouts: 24.8 us -> 0 us
  between operations: 14.7 us -> 0.86 us
    psum x4 -> x0, waiting for transfers between devices: 299 us -> none  [the longest x1 88.4 us: local(): middle = inputs + lax.psum(branch_part, 'tp')]
    reduce_scatter x4 -> x0, waiting for transfers between devices: 291 us -> none  [the longest x1 79.6 us: local(): lax.psum_scatter(down_grad, 'dp', scatter_dimension=1, tiled=True)]
    dot_general x68 -> x0, matrix products: 176 us -> none  [the longest x8 21 us: head_backward(): jnp.einsum('sqd,skd->sqk', query_rows, key_rows, preferred_element_type=j...]
    pallas_call x0 -> x2, Pallas kernels: none -> 162 us  [the longest x1 157 us: local(): pl.pallas_call(functools.partial(layer_kernel, dp), out_shape=(S((rows, w...]
    reduce_sum x16 -> x0, other arithmetic: 28.2 us -> none  [the longest x3 9.37 us: layer_norm(): centre = values - jnp.mean(values, axis=-1, keepdims=True)]
    unnamed x10 -> x0, waiting for transfers between devices: 24.3 us -> none
    convert_element_type x11 -> x0, other arithmetic: 21.3 us -> none  [the longest x8 9.1 us: head_backward(): grad_scores = (probs * (grad_probs - inner)).astype(jnp.bfloat16)]
    unnamed x58 -> x0, local copies, waits for them, and re-layouts: 10.8 us -> none
  transfers between devices with their start and end apart: 9 -> 0, of which waited for: 9 -> 0; matrix products, arithmetic and copies ran while one was open for 5% -> 0% of each run, Pallas kernels for 0% -> 0%
where the time goes in v1:
time: 166 us; the launch traced here: 163 us
  Pallas kernels  162 us (98%)
    pallas_call x1, Pallas kernels, local(): pl.pallas_call(functools.partial(layer_kernel, dp), out_shape=(S((rows, w...  157 us
    pallas_call x1, Pallas kernels, local(): pl.pallas_call(collect_kernel, out_shape=tuple((S(a.shape, a.dtype) for a...  4.78 us

profile of v1, /device:TPU:0, one launch (start us, length us, event | category | flops | bytes accessed | tf_op | source)
XLA Modules:
  0.0 163.0 jit_solution(15496485792720117481)
XLA Ops:
  0.6 157.4 %layer.1 = (bf16[1024,768]{1,0:T(8,128)(2,1)}, bf16[1024,768]{1,0:T(8,128)(2,1)}, f32[3,48,384]{2,1,0:T(8,128)}, f32[48,384]{1,0:T(8,128)}, f32[48,1536]{1,0:T(8...) custom-call(bf16[1024,768]{1,0:T(8,128)(2,1)} %x_hbm.1, bf16[1024,768]{1,0:T(8,128)(2,1)} %c_hbm.1, s32[8,128]{1,0:T(8,128)} %bitcast.6, ...), custom_call_target="tpu_custom_call" | custom-call | tf_op jit(solution)/shard_map/layer/pallas_call | solution.py:607
  158.1 4.8 %collect.1 = (bf16[1024,768]{1,0:T(8,128)(2,1)}, bf16[1024,768]{1,0:T(8,128)(2,1)}, f32[3,48,384]{2,1,0:T(8,128)}, f32[48,384]{1,0:T(8,128)}, f32[48,1536]{1,0:T...) custom-call(bf16[1024,768]{1,0:T(8,128)(2,1)} %get-tuple-element.21.refs_0_, bf16[1024,768]{1,0:T(8,128)(2,1)} %get-tuple-element.22.refs_1_, ...), custom_call_target="tpu_custom_call" | custom-call | tf_op jit(solution)/shard_map/collect/pallas_call | solution.py:684

commit v2 on v0

v2 whole, which is shorter than its diff:
```python
import functools

import jax
import jax.numpy as jnp
import numpy as np
from jax import lax
from jax.experimental import pallas as pl
from jax.experimental.pallas import tpu as pltpu
from jax.sharding import PartitionSpec as P

HD = 48
SEQ = 1024
IMG = 256
MID = SEQ // 2
HALF_IMG = IMG // 2
WIN = MID + HALF_IMG
LOW = MID - HALF_IMG
EPSILON = 1e-05
MASKED = -1e30
F32 = jnp.float32
BF16 = jnp.bfloat16
SCALE = float(HD ** (-0.5))
SCALE2 = float(HD ** (-0.5) * np.log2(np.e))
HALF_LOG2E = float(0.5 * np.log2(np.e))
INV_SQRT_2PI = 0.3989422804014327
PHI = (
    0.11962326238213554,
    0.12084553903880502,
    0.09934703796123681,
    0.13041684726157698,
    -0.05716832560524514,
    0.21011968093231104,
    -0.1593792042147725,
    0.036195106181360036,
)
TILE = 512
UNROLL = 4
UNROLL_FORWARD = 2
BANDS = ((0, 256, 0, 512), (256, 256, 0, 768), (512, 256, 256, 768), (768, 256, 512, 512))
BANDS_BACK = ((0, 256, 0, 512), (256, 256, 0, 640), (512, 128, 256, 384))
VMEM_LIMIT = 63 << 20
SEMAPHORES = 320
X, Z, ZZ, Y = range(4)
AXES = (ZZ, Z, X)
SIDE, WIDE, DEEP, HALF, NEAR, UNIT, MERGE, NORM, WIDE_HALF, DEEP_HALF = range(10)
OUT, QK, VALUE, UP, DOWN = 0, 1, 2, 3, 6
OUT_BLOCKS, QKV_BLOCKS = 6, 8
FIRST = (OUT, UP, DOWN, UP + 1, DOWN + 1)
SECOND = (UP + 2, DOWN + 2, QK, VALUE)
LOADED, PROJECTED, PREPARED, MIXED, READY, OTHER = range(6)
FORWARD, NEED, FEED, SECOND_NORM, BACK, TAIL = 10, 20, 30, 40, 50, 60


def dot(a, b, ca, cb):
    return lax.dot_general(a, b, (((ca,), (cb,)), ((), ())), preferred_element_type=F32)


def standardize(values):
    centre = values - jnp.mean(values, axis=-1, keepdims=True)
    inverse = lax.rsqrt(jnp.mean(centre * centre, axis=-1, keepdims=True) + EPSILON)
    return centre * inverse, inverse


def norm_input_grad(xh, inverse, grad, gain):
    dhg = grad * gain
    return inverse * (
        dhg - jnp.mean(dhg, axis=-1, keepdims=True) - xh * jnp.mean(dhg * xh, axis=-1, keepdims=True)
    )


def normal_parts(u):
    t = 1.0 / (1.0 + 0.3 * jnp.abs(u))
    bell = jnp.exp2(u * u * (-HALF_LOG2E))
    poly = PHI[-1]
    for coefficient in PHI[-2::-1]:
        poly = poly * t + coefficient
    tail = poly * t * bell
    return jnp.where(u >= 0, 1.0 - tail, tail), bell * INV_SQRT_2PI
ORDERS = (
    (Y, Z, X, ZZ),
    (Z, Y, X, ZZ),
    (X, Z, Y, ZZ),
    (X, Z, ZZ, Y),
    (X, Y, Z, ZZ),
    (X, Z, ZZ, Y),
)
SEQUENCE = (0, 1, 2, 3)


def back_step(n):
    return 1 - n // 2, n % 2


PLAN = {
    LOADED: ((SIDE, OUT),),
    PROJECTED: ((SIDE, UP),),
    FORWARD: ((SIDE, DOWN), (WIDE, OUT), (DEEP, OUT), (SIDE, UP + 1), (WIDE, UP), (DEEP, UP), (SIDE, DOWN + 1)),
    FORWARD + 3: ((WIDE, DOWN), (DEEP, DOWN), (HALF, OUT)),
    PREPARED: ((WIDE, UP + 1), (DEEP, UP + 1)),
    NEED: ((NEAR, OUT),),
    MIXED: ((HALF, UP), (WIDE, DOWN + 1), (DEEP, DOWN + 1), (HALF, DOWN), (HALF, UP + 1)),
    READY: ((SIDE, UP + 2),),
    FEED + 0: ((HALF, DOWN + 1), (SIDE, DOWN + 2), (WIDE, UP + 2), (DEEP, UP + 2)),
    NEED + 1: ((NEAR, UP), (NEAR, DOWN)),
    FEED + 1: ((SIDE, QK), (UNIT, 0), (SIDE, VALUE), (WIDE, DOWN + 2), (DEEP, DOWN + 2)),
    FEED + 2: ((HALF, UP + 2), (UNIT, 1)),
    NEED + 3: ((NEAR, UP + 1), (NEAR, DOWN + 1)),
    FEED + 3: ((WIDE, QK), (DEEP, QK), (UNIT, 2), (WIDE, VALUE), (DEEP, VALUE), (HALF, DOWN + 2)),
    FEED + 4: ((UNIT, 3), (HALF, QK)),
    NEED + 5: ((NEAR, UP + 2), (NEAR, DOWN + 2)),
    FEED + 5: ((UNIT, 4),),
    SECOND_NORM: ((UNIT, 5),),
    SECOND_NORM + 1: ((UNIT, 2),),
    SECOND_NORM + 2: ((HALF, VALUE), (UNIT, OUT_BLOCKS), (UNIT, OUT_BLOCKS + 1), (UNIT, 0), (UNIT, 4)),
    OTHER: ((NEAR, QK), (NEAR, VALUE)),
    BACK + 0: ((UNIT, 3), (UNIT, 5), (UNIT, OUT_BLOCKS), (UNIT, 0)),
    BACK + 1: ((UNIT, QKV_BLOCKS), (UNIT, OUT_BLOCKS + 1), (UNIT, 4), (UNIT, 0)),
    BACK + 2: ((UNIT, 5), (UNIT, QKV_BLOCKS + 1), (UNIT, OUT_BLOCKS), (UNIT, OUT_BLOCKS + 1), (UNIT, QKV_BLOCKS)),
    BACK + 3: (
        (UNIT, 2), (UNIT, QKV_BLOCKS + 2), (UNIT, 0), (UNIT, OUT_BLOCKS), (UNIT, 4), (UNIT, OUT_BLOCKS + 1),
        (UNIT, QKV_BLOCKS + 1),
    ),
    TAIL + 2: (
        (UNIT, OUT_BLOCKS), (UNIT, 2), (UNIT, 4), (UNIT, QKV_BLOCKS + 3), (NORM, 0), (UNIT, QKV_BLOCKS + 1),
        (UNIT, QKV_BLOCKS + 2), (UNIT, QKV_BLOCKS + 2), (UNIT, 2), (MERGE, 1), (UNIT, QKV_BLOCKS + 1),
        (UNIT, QKV_BLOCKS + 3), (NORM, 0), (UNIT, QKV_BLOCKS + 2), (UNIT, QKV_BLOCKS + 3), (NORM, 0),
        (UNIT, QKV_BLOCKS + 2), (UNIT, QKV_BLOCKS + 3), (NORM, 0), (UNIT, QKV_BLOCKS + 3), (NORM, 0),
    ),
}


def half_index(index, bit):
    return (index // bit) % 2


class Links:
    def __init__(self, sems, bits):
        self.sems, self.count, self.known = sems, 0, {}
        self.me, self.side = lax.axis_index("dp"), lax.axis_index("tp")
        self.bits = bits

    def semaphore(self, name, number=0, many=1):
        if name not in self.known:
            self.known[name] = self.count
            self.count += many
        return self.sems.at[self.known[name] + number]

    def partner(self, bit):
        if bit == 0:
            return {"tp": 1 - self.side}
        return {"dp": self.me + bit * (1 - 2 * half_index(self.me, bit))}

    def greet(self):
        barrier = pltpu.get_barrier_semaphore()
        for bit in self.bits:
            pl.semaphore_signal(barrier, inc=1, device_id=self.partner(bit), device_id_type=pl.DeviceIdType.MESH)

    def meet(self):
        pl.semaphore_wait(pltpu.get_barrier_semaphore(), len(self.bits))

    def send(self, name, bit, src, dst, number=0, many=1):
        return pltpu.make_async_remote_copy(
            src_ref=src,
            dst_ref=dst,
            send_sem=self.semaphore((name, 0), number, many),
            recv_sem=self.semaphore((name, 1), number, many),
            device_id=self.partner(bit),
            device_id_type=pl.DeviceIdType.MESH,
        )

    def fetch(self, name, src, dst):
        return pltpu.make_async_copy(src, dst, self.semaphore(name))


class Chunk:
    def __init__(self, links, name, bits, source, target, lead):
        self.links, self.name, self.source, self.target, self.lead = links, name, source, target, lead
        self.core_bit, self.wide_bit, self.deep_bit = bits

    def copy(self, step):
        near, wide, deep = (half_index(self.links.me, b) for b in (self.core_bit, self.wide_bit, self.deep_bit))
        rows = self.target.shape[self.lead + 2]
        lower = (rows // 2 + 15) // 16 * 16
        ahead = (slice(None),) * self.lead
        mine = (*ahead, 2 * deep + wide, near)
        first, second = pl.ds(0, lower), pl.ds(lower, rows - lower)
        bit, where = {
            SIDE: (0, mine),
            WIDE: (self.wide_bit, mine),
            DEEP: (self.deep_bit, mine),
            WIDE_HALF: (self.wide_bit, (*ahead, 2 * (1 - deep) + wide, near, second)),
            DEEP_HALF: (self.deep_bit, (*ahead, 2 * deep + 1 - wide, near, first)),
            NEAR: (self.core_bit, (*ahead, slice(None), near)),
        }[step]
        source = self.source if step == SIDE else self.target
        return self.links.send((step, self.name), bit, source.at[where], self.target.at[where])

    def act(self, step):
        if step == SIDE:
            self.copy(SIDE).wait()
            self.copy(WIDE).start()
            self.copy(DEEP).start()
        elif step == WIDE:
            self.copy(WIDE).wait()
            self.copy(DEEP_HALF).start()
        elif step == DEEP:
            self.copy(DEEP).wait()
            self.copy(WIDE_HALF).start()
        elif step == HALF:
            self.copy(WIDE_HALF).wait()
            self.copy(DEEP_HALF).wait()
            self.copy(NEAR).start()
        else:
            self.copy(NEAR).wait()


class Block:
    def __init__(self, links, name, order, bits, held, arrival, first, kept, store):
        self.links, self.name, self.order, self.bits, self.held, self.arrival = links, name, order, bits, held, arrival
        self.first, self.kept, self.store = first, kept, store
        self.done, self.rank, self.meeting = -1, 0, None

    def axes(self, rank):
        return [axis for axis in self.order if axis != Y][:rank]

    def cut(self, axis, rank, other):
        left = [a for a in AXES if a not in self.axes(rank)]
        side = half_index(self.links.me, self.bits[axis])
        return (slice(None),) * left.index(axis) + (1 - side if other else side,)

    def copy(self, axis, rank):
        source = self.held[rank].at[self.cut(axis, rank, True)]
        return self.links.send((UNIT, self.name, axis), self.bits[axis], source, self.held[rank + 1])

    def act(self):
        axis = self.order[self.done] if self.done >= 0 else None
        last = self.done == 3
        if axis is None:
            self.first.wait()
            self.held[0][...] += self.kept()
        elif axis == Y:
            self.meeting.wait()
            here, there = self.held[self.rank], self.arrival
        else:
            self.copy(axis, self.rank).wait()
            here, there = self.held[self.rank + 1], self.held[self.rank].at[self.cut(axis, self.rank, False)]
            self.rank += 1
        if axis is not None:
            if last and self.store is not None:
                self.store(here[...].astype(F32) + there[...].astype(F32))
            else:
                here[...] += there[...]
        self.done += 1
        if self.done == 4:
            return
        axis = self.order[self.done]
        if axis != Y:
            self.copy(axis, self.rank).start()
        elif self.arrival is None:
            self.meeting.start()


def pair_up(links, name, keeps, gives):
    rank = keeps.order.index(Y)
    meeting = links.send((UNIT, name, Y), 0, gives.held[rank], keeps.arrival)
    keeps.meeting = gives.meeting = meeting


def arrival_shape(order):
    before = order[: order.index(Y)]
    return [2] * (3 - len(before))


def layer_kernel(
    dp,
    x_hbm, c_hbm, ids_hbm, g1_hbm, b1_hbm, g2_hbm, b2_hbm, qkv_hbm, ow_hbm, up_hbm, dw_hbm,
    out_hbm, ig_hbm, qg_ref, pgt_ref, ug_ref, dgt_ref, ng_ref,
    sems, wq, wo, wu, wd, g1, b1, g2, b2, ids_ref, xw, cw, na_full, nat, jt, mixt, lses, lse_full,
    bias, nbt, ct, gmt, mid, acc, gacc, shared_in, shared_out, norms, g_unit, g_out, g_qkv, *landings,
):
    top = dp // 16
    near_bits = (1, 2, 4)
    c_bit = top
    axis_bits = {X: 2 * top, Z: 4 * top, ZZ: 8 * top}
    links = Links(sems, [0] + sorted({*near_bits, c_bit, *axis_bits.values()}))
    links.greet()
    me, side = links.me, links.side
    rows_all, width = xw.shape
    heads_width = jt.shape[2]
    tiles = wd.shape[1]
    heads = heads_width // HD
    first = pl.multiple_of(LOW * side, 128)
    window = pl.ds(first, WIN)
    window_there = pl.ds(pl.multiple_of(LOW * (1 - side), 128), WIN)
    at_c = half_index(me, c_bit)

    feed_rows = pl.ds(pl.multiple_of(MID * side, 128), MID)
    feed_in_window = pl.ds(pl.multiple_of(HALF_IMG * side, 128), MID)

    small = ((ids_hbm, ids_ref), (g1_hbm, g1), (b1_hbm, b1), (g2_hbm, g2), (b2_hbm, b2))
    loads = {"x": links.fetch("x", x_hbm, xw)}
    for n, (source, target) in enumerate(small):
        loads[n] = links.fetch(n, source, target)
    for j in range(3):
        loads["q", j] = links.fetch(("q", j), qkv_hbm.at[j], wq.at[0, j])
    loads["c"] = links.fetch("c", c_hbm.at[feed_rows], cw)
    late = {"o": links.fetch("o", ow_hbm, wo.at[0])}
    for tile in range(tiles):
        cols = pl.ds(tile * TILE, TILE)
        late["u", tile] = links.fetch(("u", tile), up_hbm.at[:, :, :, cols], wu.at[0, :, :, :, cols])
        late["d", tile] = links.fetch(("d", tile), dw_hbm.at[tile], wd.at[0, tile])
    for load in loads.values():
        load.start()

    chunks = {
        OUT: Chunk(links, OUT, near_bits, ow_hbm, wo.at[1], 0),
        QK: Chunk(links, QK, near_bits, qkv_hbm.at[0:2], wq.at[1, 0:2], 1),
        VALUE: Chunk(links, VALUE, near_bits, qkv_hbm.at[2], wq.at[1, 2], 0),
    }
    for tile in range(tiles):
        cols = pl.ds(tile * TILE, TILE)
        name = UP + tile
        chunks[name] = Chunk(links, name, near_bits, up_hbm.at[:, :, :, cols], wu.at[1, :, :, :, cols], 0)
        name = DOWN + tile
        chunks[name] = Chunk(links, name, near_bits, dw_hbm.at[tile], wd.at[1, tile], 0)

    blocks = {}
    merges = [None, None]
    norm_count = [0]

    def run(point):
        for action, which in PLAN.get(point, ()):
            if action == UNIT:
                blocks[which].act()
            elif action == MERGE:
                merges[which]()
            elif action == NORM:
                norm_step()
            else:
                chunks[which].act(action)

    links.meet()
    for name in FIRST:
        chunks[name].copy(SIDE).start()

    for n in range(len(small)):
        loads[n].wait()
    ids = ids_ref[...]
    columns = ids.T
    row_ids = jnp.concatenate([ids[i : i + 1] for i in range(rows_all // 128)], axis=1)
    column_ids = jnp.concatenate([columns[:, i : i + 1] for i in range(rows_all // 128)], axis=0)
    low = side == 0
    middle_id = ids[MID // 128 : MID // 128 + 1, 0:1]
    begins = jnp.sum(jnp.where(ids < middle_id, 1.0, 0.0), axis=(0, 1), keepdims=True)
    ends = jnp.sum(jnp.where(ids <= middle_id, 1.0, 0.0), axis=(0, 1), keepdims=True)
    split = jnp.where(MID - begins <= ends - MID, begins, ends)
    sign = jnp.where(low, 1.0, -1.0)
    position = lax.broadcasted_iota(jnp.int32, (1, WIN), 1).astype(F32) + (LOW * side).astype(F32)
    owned_row = jnp.where((position + 0.5 - split) * sign < 0, 1.0, 0.0)

    half_tile = 2 * HALF_IMG
    biases = (
        (acc.at[0:MID, 0:half_tile],),
        (gacc.at[0:MID, 0:half_tile], gacc.at[0:half_tile, half_tile : 2 * half_tile]),
        (mid.at[0:MID, 0:half_tile], mid.at[0:half_tile, half_tile : 2 * half_tile]),
        (acc.at[0:MID, half_tile : 2 * half_tile],),
    )
    for parts, (t0, tn, s0, sn) in zip(biases, BANDS):
        for part in parts:
            s1 = s0 + part.shape[0]
            part[...] = jnp.where(column_ids[s0:s1] == row_ids[:, t0 : t0 + tn], 0.0, MASKED)
            s0 = s1

    def row(ref):
        return ref[...].reshape(1, width)

    def weight(ref):
        value = ref[...]
        return value.reshape(-1, value.shape[-1])

    def in_unit(index):
        return g_unit.at[index // 2, index % 2]

    def head_at(ref, head):
        return ref.at[head // 4, (head // 2) % 2, head % 2]

    pairs = heads // 2

    def mixed_copy(pair):
        here = in_unit(3).at[pair // 2, pair % 2, :, :, window_there]
        return links.send("m", 0, here, mixt.at[pl.ds(heads + 2 * pair, 2)], number=pair, many=pairs)

    lse_copy = links.send("l", 0, lse_full.at[:, :, window_there], lses.at[pl.ds(heads, heads)])

    def attend(head):
        q = head_at(in_unit(0), head)[...]
        k = head_at(in_unit(1), head)[...].T
        v = jnp.concatenate([head_at(in_unit(2), head)[...], jnp.ones((16, rows_all), BF16)], axis=0)
        for parts, (t0, tn, s0, sn) in zip(biases, BANDS):
            added = jnp.concatenate([part[...] for part in parts], axis=0)
            st = dot(k[s0 : s0 + sn], q[:, t0 : t0 + tn], 1, 0) * SCALE2 + added
            most = jnp.max(st, axis=0, keepdims=True)
            expo = jnp.exp2(st - most)
            res = dot(expo.astype(BF16), v[:, s0 : s0 + sn], 0, 1).T
            total = res[HD : HD + 1]
            head_at(in_unit(3), head)[:, t0 : t0 + tn] = (res[:HD] * (1.0 / total)).astype(BF16)
            lse_full[head, :, t0 : t0 + tn] = most + jnp.log2(total)

    loads["x"].wait()
    xh, unused = standardize(xw[...].astype(F32))
    na_full[...] = (xh * row(g1) + row(b1)).astype(BF16)
    for j in range(3):
        loads["q", j].wait()
    run(LOADED)
    for j in range(3):
        part = dot(weight(wq.at[0, j]), na_full[...], 0, 1).astype(BF16)
        in_unit(j)[...] = part.reshape(2, 2, 2, HD, rows_all)
    for load in late.values():
        load.start()
    run(PROJECTED)
    for head in range(heads // 2):
        attend(head)
    for pair in range(pairs // 2):
        mixed_copy(pair).start()
    run(FORWARD)

    @pl.loop(pairs // 2, pairs)
    def _(pair):
        attend(2 * pair)
        attend(2 * pair + 1)
        mixed_copy(pair).start()
        for number in range(pairs // 2, pairs):

            @pl.when(pair == number)
            def _():
                run(FORWARD + number)

    lse_copy.start()
    for name in SECOND:
        chunks[name].copy(SIDE).start()
    loads["c"].wait()
    ct[...] = cw[...].T
    nat[...] = na_full[window, :].T
    row_ids = jnp.where(low, row_ids[:, :WIN], row_ids[:, LOW:])
    column_ids = jnp.where(low, column_ids[:WIN], column_ids[LOW:])
    bias[...] = jnp.where(column_ids == row_ids, 0.0, MASKED)
    for j in range(3):
        jt[0, j] = in_unit(j)[:, :, :, :, window].reshape(heads_width, WIN)
    mixt[0:heads] = in_unit(3)[:, :, :, :, window].reshape(heads, HD, WIN)
    lses[0:heads] = lse_full[:, :, window]
    run(PREPARED)
    run(NEED)
    late["o"].wait()
    for pair in range(pairs):
        mixed_copy(pair).wait()
    lse_copy.wait()
    run(MIXED)

    def mixed_rows(half):
        return mixt[half * heads : (half + 1) * heads, :, feed_in_window].reshape(heads_width, MID)

    fed = na_full.at[0:MID]
    middle = mid.at[feed_in_window]
    branch = dot(mixed_rows(0), weight(wo.at[0]), 0, 0) + dot(mixed_rows(1), weight(wo.at[1]), 0, 0)
    acc[...] = xw[feed_rows, :].astype(F32) + branch
    middle[...] = acc[...]
    xh, unused = standardize(acc[...])
    fed[...] = (xh * row(g2) + row(b2)).astype(BF16)
    nbt[...] = fed[...].T
    gacc[...] = jnp.zeros_like(gacc)
    for key, load in late.items():
        if key != "o":
            load.wait()

    unit = g_unit.shape[-1]
    f0, landings = landings[0], list(landings[1:])
    grid = (2, 2, 2, 2, width // 16)

    def block(name, pair, keeps, first_copy, kept, store, held0=None):
        held = [held0] if held0 is not None else [landings.pop(0)]
        held += [landings.pop(0) for _ in range(3)]
        arrival = landings.pop(0) if keeps else None
        blocks[name] = Block(
            links, name, ORDERS[pair], axis_bits, held, arrival, first_copy, kept, store if keeps else None
        )

    def unit_copy(u):
        return links.send("g", c_bit, g_unit.at[u % 2, :, :, :, 1 - at_c], f0.at[u], number=u, many=2 * tiles)

    def unit_store(tile, total):
        cols = slice(tile * TILE, (tile + 1) * TILE)
        ug_ref[:, cols] = total[:, :TILE]
        dgt_ref[:, cols] = total[:, TILE:]

    def out_copy(half):
        return links.send("h", c_bit, g_out.at[half, :, :, :, 1 - at_c], blocks[OUT_BLOCKS + half].held[0], half, 2)

    def out_store(total):
        pgt_ref[...] = total

    columns_back = UNROLL * HD

    def qkv_copy(g):
        return links.send("k", c_bit, g_qkv.at[SEQUENCE.index(g) % 2, :, :, :, 1 - at_c], blocks[QKV_BLOCKS + g].held[0], g, 4)

    def qkv_store(group, total):
        for j in range(3):
            cols = slice(j * columns_back, (j + 1) * columns_back)
            qg_ref[j, :, group * columns_back : (group + 1) * columns_back] = total[:, cols]

    for u in range(2 * tiles):
        kept = functools.partial(lambda u: g_unit[u % 2, :, :, :, at_c], u)
        store = functools.partial(unit_store, u // 2)
        block(u, u // 2, u % 2 == 0, unit_copy(u), kept, store, f0.at[u])
    for half in range(2):
        kept = functools.partial(lambda half: g_out[half, :, :, :, at_c], half)
        block(OUT_BLOCKS + half, tiles, half == 0, None, kept, out_store)
        blocks[OUT_BLOCKS + half].first = out_copy(half)
    for g in range(4):
        kept = functools.partial(lambda slot: g_qkv[slot, :, :, :, at_c], SEQUENCE.index(g) % 2)
        block(QKV_BLOCKS + g, tiles + 1 + g % 2, g >= 2, None, kept, functools.partial(qkv_store, g % 2))
        blocks[QKV_BLOCKS + g].first = qkv_copy(g)
    for tile in range(tiles):
        pair_up(links, tile, blocks[2 * tile], blocks[2 * tile + 1])
    pair_up(links, tiles, blocks[OUT_BLOCKS], blocks[OUT_BLOCKS + 1])
    for g in range(2):
        pair_up(links, tiles + 1 + g, blocks[QKV_BLOCKS + g + 2], blocks[QKV_BLOCKS + g])

    run(READY)

    @pl.loop(0, 2 * tiles)
    def _(u):
        half, tile = u % 2, u // 2
        cols = pl.ds(pl.multiple_of(tile * TILE, TILE), TILE)
        for number in range(1, 2 * tiles, 2):

            @pl.when(u == number)
            def _():
                run(NEED + number)

        up = weight(wu.at[half, :, :, :, cols])
        down = weight(wd.at[half, tile])
        hid = dot(fed[...], up, 1, 0)
        grad_active = dot(cw[...], down, 1, 1)
        phi_sum, phi = normal_parts(hid)
        active = (hid * phi_sum).astype(BF16)
        grad_hidden = (grad_active * (phi_sum + hid * phi)).astype(BF16)
        slot = u % 2
        g_unit[slot, :, :, :, :, :, TILE:] = dot(ct[...], active, 1, 0).astype(BF16).reshape(*grid, TILE)
        g_unit[slot, :, :, :, :, :, :TILE] = dot(nbt[...], grad_hidden, 1, 0).astype(BF16).reshape(*grid, TILE)
        unit_copy(u).start()
        acc[...] += dot(active, down, 1, 0)
        gacc[...] += dot(grad_hidden, up, 1, 1)
        for number in range(2 * tiles):

            @pl.when(u == number)
            def _():
                run(FEED + number)

    fed[...] = acc[...].astype(BF16)
    xh, inverse = standardize(middle[...])
    grad = gacc[...]
    norms[0, 2:3, :] = jnp.sum(grad * xh, axis=0, keepdims=True)
    norms[0, 3:4, :] = jnp.sum(grad, axis=0, keepdims=True)
    middle[...] = cw[...].astype(F32) + norm_input_grad(xh, inverse, grad, row(g2))
    cw[...] = middle[...].astype(BF16)
    edge_here = pl.ds(pl.multiple_of((MID - HALF_IMG) - 2 * HALF_IMG * side, 128), HALF_IMG)
    edge_there = pl.ds(pl.multiple_of(MID * side, 128), HALF_IMG)
    other_edge = pl.ds(pl.multiple_of(MID * (1 - side), 128), HALF_IMG)
    for half in range(2):
        part = slice(half * heads_width, (half + 1) * heads_width)
        gmt[part, feed_in_window] = dot(weight(wo.at[half]), cw[...], 1, 1).astype(BF16)
    edge_copies = []
    for half in range(2):
        here, there = (pl.ds(n * heads_width, heads_width) for n in (half, 1 - half))
        edge_copies.append(links.send("e", 0, gmt.at[here, edge_here], gmt.at[there, edge_there], number=half, many=2))
    out_copies = [
        links.send("r", 0, fed, out_hbm.at[feed_rows]),
        links.fetch("s", fed, out_hbm.at[feed_rows]),
    ]
    for copy in edge_copies + out_copies:
        copy.start()
    run(SECOND_NORM)
    ct[...] = cw[...].T
    for half in range(2):
        g_out[half] = dot(ct[...], mixed_rows(half), 1, 1).astype(BF16).reshape(*grid, heads_width)
        out_copy(half).start()
    run(SECOND_NORM + 1)
    for copy in edge_copies:
        copy.wait()
    gmt[...] = (gmt[...].astype(F32) * owned_row).astype(BF16)
    mid[other_edge, :] = jnp.zeros((HALF_IMG, width), F32)
    run(SECOND_NORM + 2)

    def attend_back(half, group):
        for u in range(UNROLL):
            head = group * UNROLL + u
            rows = pl.ds(pl.multiple_of(head * HD, 16), HD)
            out_rows = pl.ds(pl.multiple_of(half * heads_width + head * HD, 16), HD)
            q = jt[half, 0, rows, :]
            k = jt[half, 1, rows, :]
            v = jt[half, 2, rows, :]
            do = gmt[out_rows, :]
            mixed = mixt[half * heads + head]
            delta = jnp.sum(do.astype(F32) * mixed.astype(F32), axis=0, keepdims=True)
            lse = lses[half * heads + head]
            kt, vt = k.T, v.T
            grads = []
            for s0, sn, t0, tn in BANDS_BACK:
                ss, ts = slice(s0, s0 + sn), slice(t0, t0 + tn)
                st = dot(kt[ss], q[:, ts], 1, 0) * SCALE2 + (bias[ss, ts] - lse[:, ts])
                p = jnp.exp2(st)
                dprobs = dot(vt[ss], do[:, ts], 1, 0)
                ds = (p * (dprobs - delta[:, ts])).astype(BF16)
                grads.append(ds)
                jt[half, 2, rows, ss] = dot(p.astype(BF16), do[:, ts], 1, 1).astype(BF16).T
                jt[half, 1, rows, ss] = (dot(ds, q[:, ts], 1, 1) * SCALE).astype(BF16).T
            for q0, qn, unused, unused in BANDS_BACK:
                total = None
                for ds, (s0, sn, t0, tn) in zip(grads, BANDS_BACK):
                    if t0 <= q0 and q0 + qn <= t0 + tn:
                        part = dot(ds[:, q0 - t0 : q0 - t0 + qn], k[:, s0 : s0 + sn], 0, 1)
                        total = part if total is None else total + part
                jt[half, 0, rows, q0 : q0 + qn] = (total * SCALE).astype(BF16).T

    def weight_grad(n):
        half, group = back_step(n)
        rows = pl.ds(pl.multiple_of(group * columns_back, 16), columns_back)
        grads = jnp.concatenate([jt[half, j, rows, :] for j in range(3)], axis=0)
        g_qkv[n % 2] = dot(nat[...], grads, 1, 1).astype(BF16).reshape(*grid, 3 * columns_back)

    first_other = min(SEQUENCE.index(0), SEQUENCE.index(1))

    @pl.loop(0, 4)
    def _(n):
        @pl.when(n == first_other)
        def _():
            run(OTHER)
            for j in range(3):
                jt[1, j] = dot(weight(wq.at[1, j]), nat[...], 0, 0).astype(BF16)

        attend_back(*back_step(n))

        @pl.when(n < 3)
        def _():
            weight_grad(n)

        for number in range(4):

            @pl.when(n == number)
            def _():
                if number < 3:
                    qkv_copy(SEQUENCE[number]).start()
                run(BACK + number)

    for copy in out_copies:
        copy.wait()
    na = na_full.at[0:WIN]
    common_rows = pl.multiple_of(LOW * (1 - side), 128), WIN - LOW
    single_rows = pl.multiple_of((WIN - LOW) * side, 128), LOW
    common, single = pl.ds(*common_rows), pl.ds(*single_rows)
    single_there = pl.ds(pl.multiple_of(WIN * side, 128), LOW)
    ig_common = links.send("i", 0, na.at[common], shared_in)
    ig_copies = [
        links.send("j", 0, na.at[single], ig_hbm.at[single_there]),
        links.fetch("t", na.at[single], ig_hbm.at[single_there]),
        links.fetch("v", shared_out, ig_hbm.at[pl.ds(LOW, WIN - LOW)]),
    ]

    def merge():
        ig_common.wait()
        shared_out[...] = na[common, :] + shared_in[...]
        ig_copies[2].start()

    merges[1] = merge

    def input_grad(start, count):
        rows = pl.ds(start, count)
        grad = None
        for half in range(2):
            for j in range(3):
                part = dot(jt[half, j, :, rows], weight(wq.at[half, j]), 0, 1)
                grad = part if grad is None else grad + part
        xh, inverse = standardize(xw[pl.ds(pl.multiple_of(first + start, 128), count), :].astype(F32))
        na[rows, :] = (mid[rows, :] + norm_input_grad(xh, inverse, grad, row(g1))).astype(BF16)
        return jnp.sum(grad * xh, axis=0, keepdims=True), jnp.sum(grad, axis=0, keepdims=True)

    norm_bits = (c_bit, *axis_bits.values(), 0)

    def norm_copy(n):
        return links.send("w", norm_bits[n], norms.at[2 * n], norms.at[2 * n + 1], number=n, many=5)

    def norm_step():
        n = norm_count[0]
        norm_count[0] += 1
        norm_copy(n).wait()
        norms[2 * n + 2] = norms[2 * n] + norms[2 * n + 1]
        if n < 4:
            norm_copy(n + 1).start()

    gain_one, shift_one = input_grad(*common_rows)
    ig_common.start()
    run(TAIL)
    weight_grad(3)
    qkv_copy(SEQUENCE[3]).start()
    run(TAIL + 1)
    gain_two, shift_two = input_grad(*single_rows)
    for copy in ig_copies[:2]:
        copy.start()
    norms[0, 0:1, :] = gain_one + gain_two
    norms[0, 1:2, :] = shift_one + shift_two
    norms[0, 4:8, :] = jnp.zeros((4, width), F32)
    norm_copy(0).start()
    run(TAIL + 2)
    ng_ref[...] = norms[10]
    for copy in ig_copies:
        copy.wait()


def collect_kernel(*refs):
    count = (len(refs) - 3) // 3
    sources, norms, targets = refs[:count], refs[count], refs[count + 1 : 2 * count + 1]
    target, held, sems = refs[2 * count + 1], refs[2 * count + 2 : 3 * count + 2], refs[-1]
    loads = [pltpu.make_async_copy(a, b, sems.at[0, n]) for n, (a, b) in enumerate(zip(sources, held))]
    stores = [pltpu.make_async_copy(a, b, sems.at[1, n]) for n, (a, b) in enumerate(zip(held, targets))]
    for load in loads:
        load.start()
    rows, share = target.shape
    width = norms.shape[1]
    place = lax.broadcasted_iota(jnp.int32, (width, share), 0) - share * lax.axis_index("dp")
    pick = jnp.where(place == lax.broadcasted_iota(jnp.int32, (width, share), 1), 1.0, 0.0)
    target[...] = lax.dot_general(
        norms[...], pick, (((1,), (0,)), ((), ())), precision=lax.Precision.HIGHEST, preferred_element_type=F32
    )[:rows]
    for load, store in zip(loads, stores):
        load.wait()
        store.start()
    for store in stores:
        store.wait()


def local(
    dp,
    block_input,
    segment_ids,
    gain_one,
    shift_one,
    qkv_weight,
    out_weight,
    gain_two,
    shift_two,
    up_weight,
    down_weight,
    out_cotangent,
):
    rows, width = block_input.shape
    heads_width, hidden = out_weight.shape[0], up_weight.shape[1]
    block, unit, group, tiles = width // 16, 2 * TILE, 3 * UNROLL * HD, hidden // TILE
    heads = heads_width // HD
    S, V = jax.ShapeDtypeStruct, pltpu.VMEM
    place = pl.BlockSpec(memory_space=pltpu.VMEM)
    far = pl.BlockSpec(memory_space=pl.ANY)
    halves = [2, 2, 2, 2]
    landings = [V((2 * tiles, *halves[1:], block, unit), BF16)]
    kinds = [(u // 2, u % 2 == 0, unit, False) for u in range(2 * tiles)]
    kinds += [(tiles, half == 0, heads_width, True) for half in range(2)]
    kinds += [(tiles + 1 + g % 2, g >= 2, group, True) for g in range(4)]
    for pair, keeps, wide, whole in kinds:
        landings += [V((*halves[n:], block, wide), BF16) for n in range(1 if whole else 2, 5)]
        if keeps:
            landings.append(V((*arrival_shape(ORDERS[pair]), block, wide), BF16))
    out, ig, qg, pgt, ug, dgt, ng = pl.pallas_call(
        functools.partial(layer_kernel, dp),
        out_shape=(
            S((rows, width), BF16),
            S((rows, width), BF16),
            S((3, block, heads_width), F32),
            S((block, heads_width), F32),
            S((block, hidden), F32),
            S((block, hidden), F32),
            S((8, width), F32),
        ),
        in_specs=[far] * 11,
        out_specs=[far, far] + [place] * 5,
        scratch_shapes=[
            pltpu.SemaphoreType.DMA((SEMAPHORES,)),
            V((2, 3, 4, 2, width // 8, heads_width), BF16),
            V((2, 4, 2, heads_width // 8, width), BF16),
            V((2, 4, 2, width // 8, hidden), BF16),
            V((2, tiles, 4, 2, TILE // 8, width), BF16),
            *[V((width,), F32)] * 4,
            V((rows // 128, 128), jnp.int32),
            V((rows, width), BF16),
            V((MID, width), BF16),
            V((rows, width), BF16),
            V((width, WIN), BF16),
            V((2, 3, heads_width, WIN), BF16),
            V((2 * heads, HD, WIN), BF16),
            V((2 * heads, 1, WIN), F32),
            V((heads, 1, rows), F32),
            V((WIN, WIN), F32),
            V((width, MID), BF16),
            V((width, MID), BF16),
            V((width, WIN), BF16),
            V((WIN, width), F32),
            V((MID, width), F32),
            V((MID, width), F32),
            V((WIN - LOW, width), BF16),
            V((WIN - LOW, width), BF16),
            V((11, 8, width), F32),
            V((2, *halves, block, unit), BF16),
            V((2, *halves, block, heads_width), BF16),
            V((2, *halves, block, group), BF16),
            *landings,
        ],
        compiler_params=pltpu.CompilerParams(
            vmem_limit_bytes=VMEM_LIMIT, collective_id=0, has_side_effects=True
        ),
        name="layer",
    )(
        block_input,
        out_cotangent,
        segment_ids.reshape(rows // 128, 128),
        gain_one,
        shift_one,
        gain_two,
        shift_two,
        qkv_weight.transpose(1, 0, 2).reshape(3, 4, 2, width // 8, heads_width),
        out_weight.reshape(4, 2, heads_width // 8, width),
        up_weight.reshape(4, 2, width // 8, hidden),
        down_weight.reshape(tiles, 4, 2, TILE // 8, width),
    )
    rest = dp // 16
    if rest > 1:
        groups = [list(range(g * rest, (g + 1) * rest)) for g in range(16)]
        scatter = functools.partial(lax.psum_scatter, axis_name="dp", axis_index_groups=groups, tiled=True)
        qg = scatter(qg, scatter_dimension=1)
        pgt, ug, dgt = (scatter(part, scatter_dimension=0) for part in (pgt, ug, dgt))
        ng = lax.psum(ng, "dp", axis_index_groups=groups)
    share = width // dp
    results = (out, ig, qg, pgt, ug, dgt)
    out, ig, qg, pgt, ug, dgt, ng = pl.pallas_call(
        collect_kernel,
        out_shape=tuple(S(a.shape, a.dtype) for a in results) + (S((4, share), F32),),
        in_specs=[far] * 6 + [place],
        out_specs=[far] * 6 + [place],
        scratch_shapes=[V(a.shape, a.dtype) for a in results] + [pltpu.SemaphoreType.DMA((2, 6))],
        name="collect",
    )(*results, ng)
    return out, ig, qg.transpose(1, 0, 2), pgt.T, ug, dgt.T, ng


def solution(mesh):
    in_specs = (
        P("dp", None),
        P("dp"),
        P(),
        P(),
        P(None, None, "tp"),
        P("tp", None),
        P(),
        P(),
        P(None, "tp"),
        P("tp", None),
        P("dp", None),
    )
    out_specs = (
        P("dp", None),
        P("dp", None),
        P("dp", None, "tp"),
        P("tp", "dp"),
        P("dp", "tp"),
        P("tp", "dp"),
        P(None, "dp"),
    )
    step = functools.partial(local, mesh.shape["dp"])
    return jax.shard_map(step, mesh=mesh, in_specs=in_specs, out_specs=out_specs, check_vma=False)
```

time: 895 us -> 135 us (0.15)
  waiting for transfers between devices: 614 us -> 0 us
  matrix products: 176 us -> 0 us
  Pallas kernels: 0 us -> 134 us
  other arithmetic: 55.6 us -> 0 us
  local copies, waits for them, and re-layouts: 24.8 us -> 0 us
  between operations: 14.7 us -> 0.85 us
    psum x4 -> x0, waiting for transfers between devices: 299 us -> none  [the longest x1 88.4 us: local(): middle = inputs + lax.psum(branch_part, 'tp')]
    reduce_scatter x4 -> x0, waiting for transfers between devices: 291 us -> none  [the longest x1 79.6 us: local(): lax.psum_scatter(down_grad, 'dp', scatter_dimension=1, tiled=True)]
    dot_general x68 -> x0, matrix products: 176 us -> none  [the longest x8 21 us: head_backward(): jnp.einsum('sqd,skd->sqk', query_rows, key_rows, preferred_element_type=j...]
    pallas_call x0 -> x2, Pallas kernels: none -> 134 us  [the longest x1 129 us: local(): pl.pallas_call(functools.partial(layer_kernel, dp), out_shape=(S((rows, w...]
    reduce_sum x16 -> x0, other arithmetic: 28.2 us -> none  [the longest x3 9.37 us: layer_norm(): centre = values - jnp.mean(values, axis=-1, keepdims=True)]
    unnamed x10 -> x0, waiting for transfers between devices: 24.3 us -> none
    convert_element_type x11 -> x0, other arithmetic: 21.3 us -> none  [the longest x8 9.1 us: head_backward(): grad_scores = (probs * (grad_probs - inner)).astype(jnp.bfloat16)]
    unnamed x58 -> x0, local copies, waits for them, and re-layouts: 10.8 us -> none
  transfers between devices with their start and end apart: 9 -> 0, of which waited for: 9 -> 0; matrix products, arithmetic and copies ran while one was open for 5% -> 0% of each run, Pallas kernels for 0% -> 0%
where the time goes in v2:
time: 135 us; the launch traced here: 134 us
  Pallas kernels  134 us (99%)
    pallas_call x1, Pallas kernels, local(): pl.pallas_call(functools.partial(layer_kernel, dp), out_shape=(S((rows, w...  129 us
    pallas_call x1, Pallas kernels, local(): pl.pallas_call(collect_kernel, out_shape=tuple((S(a.shape, a.dtype) for a...  4.78 us

profile of v2, /device:TPU:0, one launch (start us, length us, event | category | flops | bytes accessed | tf_op | source)
XLA Modules:
  0.0 134.4 jit_solution(10375823862660064414)
XLA Ops:
  0.6 128.8 %layer.1 = (bf16[1024,768]{1,0:T(8,128)(2,1)}, bf16[1024,768]{1,0:T(8,128)(2,1)}, f32[3,48,384]{2,1,0:T(8,128)}, f32[48,384]{1,0:T(8,128)}, f32[48,1536]{1,0:T(8...) custom-call(bf16[1024,768]{1,0:T(8,128)(2,1)} %x_hbm.1, bf16[1024,768]{1,0:T(8,128)(2,1)} %c_hbm.1, s32[8,128]{1,0:T(8,128)} %bitcast.14, ...), custom_call_target="tpu_custom_call" | custom-call | tf_op jit(solution)/shard_map/layer/pallas_call | solution.py:772
  129.4 4.8 %collect.1 = (bf16[1024,768]{1,0:T(8,128)(2,1)}, bf16[1024,768]{1,0:T(8,128)(2,1)}, f32[3,48,384]{2,1,0:T(8,128)}, f32[48,384]{1,0:T(8,128)}, f32[48,1536]{1,0:T...) custom-call(bf16[1024,768]{1,0:T(8,128)(2,1)} %get-tuple-element.21.refs_0_, bf16[1024,768]{1,0:T(8,128)(2,1)} %get-tuple-element.22.refs_1_, ...), custom_call_target="tpu_custom_call" | custom-call | tf_op jit(solution)/shard_map/collect/pallas_call | solution.py:842

commit v3 on v2

--- a/solution.py
+++ b/solution.py
@@ -42,13 +42,14 @@
 SEMAPHORES = 320
 X, Z, ZZ, Y = range(4)
 AXES = (ZZ, Z, X)
-SIDE, WIDE, DEEP, HALF, NEAR, UNIT, MERGE, NORM, WIDE_HALF, DEEP_HALF = range(10)
-OUT, QK, VALUE, UP, DOWN = 0, 1, 2, 3, 6
+SIDE, WIDE, DEEP, CROSS, NEAR, UNIT, MERGE, NORM = range(8)
+OUT, QKV, UP, DOWN = 0, 1, 2, 5
 OUT_BLOCKS, QKV_BLOCKS = 6, 8
 FIRST = (OUT, UP, DOWN, UP + 1, DOWN + 1)
-SECOND = (UP + 2, DOWN + 2, QK, VALUE)
+SECOND = (UP + 2, DOWN + 2, QKV)
+NEAR_BITS = (1, 4, 2)
 LOADED, PROJECTED, PREPARED, MIXED, READY, OTHER = range(6)
-FORWARD, NEED, FEED, SECOND_NORM, BACK, TAIL = 10, 20, 30, 40, 50, 60
+FORWARD, NEED, MIDWAY, FEED, SECOND_NORM, BACK, TAIL = 10, 20, 30, 40, 50, 60, 70
 
 
 def dot(a, b, ca, cb):
@@ -78,11 +79,11 @@
     return jnp.where(u >= 0, 1.0 - tail, tail), bell * INV_SQRT_2PI
 ORDERS = (
     (Y, Z, X, ZZ),
-    (Z, Y, X, ZZ),
     (X, Z, Y, ZZ),
-    (X, Z, ZZ, Y),
+    (Z, X, Y, ZZ),
+    (X, ZZ, Z, Y),
     (X, Y, Z, ZZ),
-    (X, Z, ZZ, Y),
+    (X, Y, Z, ZZ),
 )
 SEQUENCE = (0, 1, 2, 3)
 
@@ -93,40 +94,45 @@
 
 PLAN = {
     LOADED: ((SIDE, OUT),),
-    PROJECTED: ((SIDE, UP),),
-    FORWARD: ((SIDE, DOWN), (WIDE, OUT), (DEEP, OUT), (SIDE, UP + 1), (WIDE, UP), (DEEP, UP), (SIDE, DOWN + 1)),
-    FORWARD + 3: ((WIDE, DOWN), (DEEP, DOWN), (HALF, OUT)),
-    PREPARED: ((WIDE, UP + 1), (DEEP, UP + 1)),
-    NEED: ((NEAR, OUT),),
-    MIXED: ((HALF, UP), (WIDE, DOWN + 1), (DEEP, DOWN + 1), (HALF, DOWN), (HALF, UP + 1)),
-    READY: ((SIDE, UP + 2),),
-    FEED + 0: ((HALF, DOWN + 1), (SIDE, DOWN + 2), (WIDE, UP + 2), (DEEP, UP + 2)),
+    PROJECTED: ((SIDE, UP), (SIDE, DOWN), (DEEP, OUT)),
+    FORWARD: ((SIDE, UP + 1), (DEEP, UP), (SIDE, DOWN + 1)),
+    FORWARD + 2: ((DEEP, DOWN), (CROSS, OUT)),
+    FORWARD + 3: ((DEEP, UP + 1),),
+    PREPARED: ((DEEP, DOWN + 1), (CROSS, UP)),
+    NEED + 9: ((NEAR, OUT),),
+    READY: ((CROSS, DOWN),),
+    MIDWAY + 0: ((SIDE, UP + 2),),
+    FEED + 0: ((CROSS, UP + 1), (SIDE, DOWN + 2), (CROSS, DOWN + 1)),
     NEED + 1: ((NEAR, UP), (NEAR, DOWN)),
-    FEED + 1: ((SIDE, QK), (UNIT, 0), (SIDE, VALUE), (WIDE, DOWN + 2), (DEEP, DOWN + 2)),
-    FEED + 2: ((HALF, UP + 2), (UNIT, 1)),
-    NEED + 3: ((NEAR, UP + 1), (NEAR, DOWN + 1)),
-    FEED + 3: ((WIDE, QK), (DEEP, QK), (UNIT, 2), (WIDE, VALUE), (DEEP, VALUE), (HALF, DOWN + 2)),
-    FEED + 4: ((UNIT, 3), (HALF, QK)),
-    NEED + 5: ((NEAR, UP + 2), (NEAR, DOWN + 2)),
-    FEED + 5: ((UNIT, 4),),
-    SECOND_NORM: ((UNIT, 5),),
-    SECOND_NORM + 1: ((UNIT, 2),),
-    SECOND_NORM + 2: ((HALF, VALUE), (UNIT, OUT_BLOCKS), (UNIT, OUT_BLOCKS + 1), (UNIT, 0), (UNIT, 4)),
-    OTHER: ((NEAR, QK), (NEAR, VALUE)),
-    BACK + 0: ((UNIT, 3), (UNIT, 5), (UNIT, OUT_BLOCKS), (UNIT, 0)),
-    BACK + 1: ((UNIT, QKV_BLOCKS), (UNIT, OUT_BLOCKS + 1), (UNIT, 4), (UNIT, 0)),
-    BACK + 2: ((UNIT, 5), (UNIT, QKV_BLOCKS + 1), (UNIT, OUT_BLOCKS), (UNIT, OUT_BLOCKS + 1), (UNIT, QKV_BLOCKS)),
-    BACK + 3: (
-        (UNIT, 2), (UNIT, QKV_BLOCKS + 2), (UNIT, 0), (UNIT, OUT_BLOCKS), (UNIT, 4), (UNIT, OUT_BLOCKS + 1),
-        (UNIT, QKV_BLOCKS + 1),
-    ),
+    MIDWAY + 1: ((DEEP, UP + 2),),
+    FEED + 1: ((UNIT, 0), (DEEP, DOWN + 2), (SIDE, QKV)),
+    NEED + 2: ((NEAR, UP + 1), (NEAR, DOWN + 1)),
+    FEED + 2: ((UNIT, 1), (CROSS, UP + 2)),
+    MIDWAY + 3: ((CROSS, DOWN + 2),),
+    FEED + 3: ((UNIT, 2), (DEEP, QKV)),
+    NEED + 4: ((NEAR, UP + 2), (NEAR, DOWN + 2)),
+    FEED + 4: ((UNIT, 3),),
+    FEED + 5: ((UNIT, 4), (CROSS, QKV)),
+    SECOND_NORM: ((UNIT, 5), (UNIT, 2)),
+    SECOND_NORM + 2: ((UNIT, OUT_BLOCKS), (UNIT, 0), (UNIT, OUT_BLOCKS + 1), (UNIT, 4), (UNIT, 3)),
+    OTHER: ((NEAR, QKV),),
+    BACK + 0: ((UNIT, OUT_BLOCKS), (UNIT, 5), (UNIT, OUT_BLOCKS + 1)),
+    BACK + 1: ((UNIT, 2), (UNIT, QKV_BLOCKS), (UNIT, 4)),
+    BACK + 2: ((UNIT, 5), (UNIT, QKV_BLOCKS + 1), (UNIT, 0), (UNIT, QKV_BLOCKS)),
+    BACK + 3: ((UNIT, 3), (UNIT, 3), (UNIT, QKV_BLOCKS + 2), (UNIT, 5), (UNIT, OUT_BLOCKS), (UNIT, QKV_BLOCKS + 1)),
+    TAIL: ((UNIT, OUT_BLOCKS + 1), (UNIT, QKV_BLOCKS + 3)),
+    TAIL + 1: ((UNIT, 0), (UNIT, 3)),
     TAIL + 2: (
-        (UNIT, OUT_BLOCKS), (UNIT, 2), (UNIT, 4), (UNIT, QKV_BLOCKS + 3), (NORM, 0), (UNIT, QKV_BLOCKS + 1),
-        (UNIT, QKV_BLOCKS + 2), (UNIT, QKV_BLOCKS + 2), (UNIT, 2), (MERGE, 1), (UNIT, QKV_BLOCKS + 1),
-        (UNIT, QKV_BLOCKS + 3), (NORM, 0), (UNIT, QKV_BLOCKS + 2), (UNIT, QKV_BLOCKS + 3), (NORM, 0),
-        (UNIT, QKV_BLOCKS + 2), (UNIT, QKV_BLOCKS + 3), (NORM, 0), (UNIT, QKV_BLOCKS + 3), (NORM, 0),
+        (NORM, 0), (UNIT, QKV_BLOCKS + 2), (UNIT, QKV_BLOCKS + 2), (UNIT, 5), (UNIT, OUT_BLOCKS),
+        (UNIT, OUT_BLOCKS + 1), (UNIT, QKV_BLOCKS + 3), (UNIT, QKV_BLOCKS + 3), (NORM, 0), (MERGE, 1), (UNIT, 0),
+        (UNIT, QKV_BLOCKS + 2), (UNIT, QKV_BLOCKS + 3), (NORM, 0), (UNIT, QKV_BLOCKS + 2), (UNIT, QKV_BLOCKS + 3),
+        (NORM, 0), (UNIT, OUT_BLOCKS), (NORM, 0),
     ),
 }
+
+
+def feed_half(u):
+    return (u + u // 2 - u // 4) % 2
 
 
 def half_index(index, bit):
@@ -179,17 +185,13 @@
 
     def copy(self, step):
         near, wide, deep = (half_index(self.links.me, b) for b in (self.core_bit, self.wide_bit, self.deep_bit))
-        rows = self.target.shape[self.lead + 2]
-        lower = (rows // 2 + 15) // 16 * 16
         ahead = (slice(None),) * self.lead
         mine = (*ahead, 2 * deep + wide, near)
-        first, second = pl.ds(0, lower), pl.ds(lower, rows - lower)
         bit, where = {
             SIDE: (0, mine),
             WIDE: (self.wide_bit, mine),
             DEEP: (self.deep_bit, mine),
-            WIDE_HALF: (self.wide_bit, (*ahead, 2 * (1 - deep) + wide, near, second)),
-            DEEP_HALF: (self.deep_bit, (*ahead, 2 * deep + 1 - wide, near, first)),
+            CROSS: (self.wide_bit, (*ahead, 2 * (1 - deep) + wide, near)),
             NEAR: (self.core_bit, (*ahead, slice(None), near)),
         }[step]
         source = self.source if step == SIDE else self.target
@@ -200,15 +202,12 @@
             self.copy(SIDE).wait()
             self.copy(WIDE).start()
             self.copy(DEEP).start()
-        elif step == WIDE:
-            self.copy(WIDE).wait()
-            self.copy(DEEP_HALF).start()
         elif step == DEEP:
             self.copy(DEEP).wait()
-            self.copy(WIDE_HALF).start()
-        elif step == HALF:
-            self.copy(WIDE_HALF).wait()
-            self.copy(DEEP_HALF).wait()
+            self.copy(CROSS).start()
+        elif step == CROSS:
+            self.copy(WIDE).wait()
+            self.copy(CROSS).wait()
             self.copy(NEAR).start()
         else:
             self.copy(NEAR).wait()
@@ -274,12 +273,12 @@
 def layer_kernel(
     dp,
     x_hbm, c_hbm, ids_hbm, g1_hbm, b1_hbm, g2_hbm, b2_hbm, qkv_hbm, ow_hbm, up_hbm, dw_hbm,
-    out_hbm, ig_hbm, qg_ref, pgt_ref, ug_ref, dgt_ref, ng_ref,
-    sems, wq, wo, wu, wd, g1, b1, g2, b2, ids_ref, xw, cw, na_full, nat, jt, mixt, lses, lse_full,
+    out_hbm, ig_hbm, qg_hbm, pgt_hbm, ug_hbm, dgt_hbm, ng_hbm,
+    sems, qg_ref, pgt_ref, ug_ref, dgt_ref, wq, wo, wu, wd, g1, b1, g2, b2, ids_ref, xw, cw, na_full, nat, jt, mixt, lses, deltas, lse_full,
     bias, nbt, ct, gmt, mid, acc, gacc, shared_in, shared_out, norms, g_unit, g_out, g_qkv, *landings,
 ):
     top = dp // 16
-    near_bits = (1, 2, 4)
+    near_bits = NEAR_BITS
     c_bit = top
     axis_bits = {X: 2 * top, Z: 4 * top, ZZ: 8 * top}
     links = Links(sems, [0] + sorted({*near_bits, c_bit, *axis_bits.values()}))
@@ -296,6 +295,7 @@
 
     feed_rows = pl.ds(pl.multiple_of(MID * side, 128), MID)
     feed_in_window = pl.ds(pl.multiple_of(HALF_IMG * side, 128), MID)
+    feed_there = pl.ds(pl.multiple_of(MID * (1 - side), 128), MID)
 
     small = ((ids_hbm, ids_ref), (g1_hbm, g1), (b1_hbm, b1), (g2_hbm, g2), (b2_hbm, b2))
     loads = {"x": links.fetch("x", x_hbm, xw)}
@@ -314,8 +314,7 @@
 
     chunks = {
         OUT: Chunk(links, OUT, near_bits, ow_hbm, wo.at[1], 0),
-        QK: Chunk(links, QK, near_bits, qkv_hbm.at[0:2], wq.at[1, 0:2], 1),
-        VALUE: Chunk(links, VALUE, near_bits, qkv_hbm.at[2], wq.at[1, 2], 0),
+        QKV: Chunk(links, QKV, near_bits, qkv_hbm, wq.at[1], 1),
     }
     for tile in range(tiles):
         cols = pl.ds(tile * TILE, TILE)
@@ -387,7 +386,7 @@
     pairs = heads // 2
 
     def mixed_copy(pair):
-        here = in_unit(3).at[pair // 2, pair % 2, :, :, window_there]
+        here = in_unit(3).at[pair // 2, pair % 2, :, :, feed_there]
         return links.send("m", 0, here, mixt.at[pl.ds(heads + 2 * pair, 2)], number=pair, many=pairs)
 
     lse_copy = links.send("l", 0, lse_full.at[:, :, window_there], lses.at[pl.ds(heads, heads)])
@@ -446,18 +445,17 @@
     bias[...] = jnp.where(column_ids == row_ids, 0.0, MASKED)
     for j in range(3):
         jt[0, j] = in_unit(j)[:, :, :, :, window].reshape(heads_width, WIN)
-    mixt[0:heads] = in_unit(3)[:, :, :, :, window].reshape(heads, HD, WIN)
+    mixt[0:heads] = in_unit(3)[:, :, :, :, feed_rows].reshape(heads, HD, MID)
     lses[0:heads] = lse_full[:, :, window]
     run(PREPARED)
-    run(NEED)
+    run(NEED + 9)
     late["o"].wait()
     for pair in range(pairs):
         mixed_copy(pair).wait()
-    lse_copy.wait()
     run(MIXED)
 
     def mixed_rows(half):
-        return mixt[half * heads : (half + 1) * heads, :, feed_in_window].reshape(heads_width, MID)
+        return mixt[half * heads : (half + 1) * heads].reshape(heads_width, MID)
 
     fed = na_full.at[0:MID]
     middle = mid.at[feed_in_window]
@@ -487,16 +485,26 @@
     def unit_copy(u):
         return links.send("g", c_bit, g_unit.at[u % 2, :, :, :, 1 - at_c], f0.at[u], number=u, many=2 * tiles)
 
+    def unit_results(tile):
+        cols = pl.ds(tile * TILE, TILE)
+        return [
+            links.fetch((tile, "u"), ug_ref.at[:, cols], ug_hbm.at[:, cols]),
+            links.fetch((tile, "d"), dgt_ref.at[:, cols], dgt_hbm.at[:, cols]),
+        ]
+
     def unit_store(tile, total):
         cols = slice(tile * TILE, (tile + 1) * TILE)
         ug_ref[:, cols] = total[:, :TILE]
         dgt_ref[:, cols] = total[:, TILE:]
+        for copy in unit_results(tile):
+            copy.start()
 
     def out_copy(half):
         return links.send("h", c_bit, g_out.at[half, :, :, :, 1 - at_c], blocks[OUT_BLOCKS + half].held[0], half, 2)
 
     def out_store(total):
         pgt_ref[...] = total
+        links.fetch("p", pgt_ref, pgt_hbm).start()
 
     columns_back = UNROLL * HD
 
@@ -511,7 +519,7 @@
     for u in range(2 * tiles):
         kept = functools.partial(lambda u: g_unit[u % 2, :, :, :, at_c], u)
         store = functools.partial(unit_store, u // 2)
-        block(u, u // 2, u % 2 == 0, unit_copy(u), kept, store, f0.at[u])
+        block(u, u // 2, feed_half(u) == 0, unit_copy(u), kept, store, f0.at[u])
     for half in range(2):
         kept = functools.partial(lambda half: g_out[half, :, :, :, at_c], half)
         block(OUT_BLOCKS + half, tiles, half == 0, None, kept, out_store)
@@ -521,7 +529,8 @@
         block(QKV_BLOCKS + g, tiles + 1 + g % 2, g >= 2, None, kept, functools.partial(qkv_store, g % 2))
         blocks[QKV_BLOCKS + g].first = qkv_copy(g)
     for tile in range(tiles):
-        pair_up(links, tile, blocks[2 * tile], blocks[2 * tile + 1])
+        pair = [blocks[2 * tile], blocks[2 * tile + 1]]
+        pair_up(links, tile, pair[feed_half(2 * tile)], pair[1 - feed_half(2 * tile)])
     pair_up(links, tiles, blocks[OUT_BLOCKS], blocks[OUT_BLOCKS + 1])
     for g in range(2):
         pair_up(links, tiles + 1 + g, blocks[QKV_BLOCKS + g + 2], blocks[QKV_BLOCKS + g])
@@ -530,9 +539,9 @@
 
     @pl.loop(0, 2 * tiles)
     def _(u):
-        half, tile = u % 2, u // 2
+        half, tile = feed_half(u), u // 2
         cols = pl.ds(pl.multiple_of(tile * TILE, TILE), TILE)
-        for number in range(1, 2 * tiles, 2):
+        for number in [v for v in range(2 * tiles) if feed_half(v)]:
 
             @pl.when(u == number)
             def _():
@@ -541,15 +550,21 @@
         up = weight(wu.at[half, :, :, :, cols])
         down = weight(wd.at[half, tile])
         hid = dot(fed[...], up, 1, 0)
-        grad_active = dot(cw[...], down, 1, 1)
         phi_sum, phi = normal_parts(hid)
         active = (hid * phi_sum).astype(BF16)
+        grad_active = dot(cw[...], down, 1, 1)
+        acc[...] += dot(active, down, 1, 0)
         grad_hidden = (grad_active * (phi_sum + hid * phi)).astype(BF16)
+        for number in range(2 * tiles):
+
+            @pl.when(u == number)
+            def _():
+                run(MIDWAY + number)
+
         slot = u % 2
         g_unit[slot, :, :, :, :, :, TILE:] = dot(ct[...], active, 1, 0).astype(BF16).reshape(*grid, TILE)
         g_unit[slot, :, :, :, :, :, :TILE] = dot(nbt[...], grad_hidden, 1, 0).astype(BF16).reshape(*grid, TILE)
         unit_copy(u).start()
-        acc[...] += dot(active, down, 1, 0)
         gacc[...] += dot(grad_hidden, up, 1, 1)
         for number in range(2 * tiles):
 
@@ -569,11 +584,18 @@
     other_edge = pl.ds(pl.multiple_of(MID * (1 - side), 128), HALF_IMG)
     for half in range(2):
         part = slice(half * heads_width, (half + 1) * heads_width)
-        gmt[part, feed_in_window] = dot(weight(wo.at[half]), cw[...], 1, 1).astype(BF16)
+        grads = dot(weight(wo.at[half]), cw[...], 1, 1).astype(BF16)
+        gmt[part, feed_in_window] = grads
+        sums = jnp.sum((grads.astype(F32) * mixed_rows(half).astype(F32)).reshape(heads, HD, MID), axis=1, keepdims=True)
+        deltas[half * heads : (half + 1) * heads, :, feed_in_window] = sums
     edge_copies = []
     for half in range(2):
         here, there = (pl.ds(n * heads_width, heads_width) for n in (half, 1 - half))
         edge_copies.append(links.send("e", 0, gmt.at[here, edge_here], gmt.at[there, edge_there], number=half, many=2))
+        here, there = (pl.ds(n * heads, heads) for n in (half, 1 - half))
+        edge_copies.append(
+            links.send("n", 0, deltas.at[here, :, edge_here], deltas.at[there, :, edge_there], number=half, many=2)
+        )
     out_copies = [
         links.send("r", 0, fed, out_hbm.at[feed_rows]),
         links.fetch("s", fed, out_hbm.at[feed_rows]),
@@ -588,6 +610,8 @@
     run(SECOND_NORM + 1)
     for copy in edge_copies:
         copy.wait()
+    lse_copy.wait()
+    deltas[...] = deltas[...] * owned_row
     gmt[...] = (gmt[...].astype(F32) * owned_row).astype(BF16)
     mid[other_edge, :] = jnp.zeros((HALF_IMG, width), F32)
     run(SECOND_NORM + 2)
@@ -601,8 +625,7 @@
             k = jt[half, 1, rows, :]
             v = jt[half, 2, rows, :]
             do = gmt[out_rows, :]
-            mixed = mixt[half * heads + head]
-            delta = jnp.sum(do.astype(F32) * mixed.astype(F32), axis=0, keepdims=True)
+            delta = deltas[half * heads + head]
             lse = lses[half * heads + head]
             kt, vt = k.T, v.T
             grads = []
@@ -619,9 +642,9 @@
                 total = None
                 for ds, (s0, sn, t0, tn) in zip(grads, BANDS_BACK):
                     if t0 <= q0 and q0 + qn <= t0 + tn:
-                        part = dot(ds[:, q0 - t0 : q0 - t0 + qn], k[:, s0 : s0 + sn], 0, 1)
+                        part = dot(k[:, s0 : s0 + sn], ds[:, q0 - t0 : q0 - t0 + qn], 1, 0)
                         total = part if total is None else total + part
-                jt[half, 0, rows, q0 : q0 + qn] = (total * SCALE).astype(BF16).T
+                jt[half, 0, rows, q0 : q0 + qn] = (total * SCALE).astype(BF16)
 
     def weight_grad(n):
         half, group = back_step(n)
@@ -698,44 +721,62 @@
         if n < 4:
             norm_copy(n + 1).start()
 
+    weight_grad(3)
+    qkv_copy(SEQUENCE[3]).start()
     gain_one, shift_one = input_grad(*common_rows)
     ig_common.start()
     run(TAIL)
-    weight_grad(3)
-    qkv_copy(SEQUENCE[3]).start()
-    run(TAIL + 1)
     gain_two, shift_two = input_grad(*single_rows)
     for copy in ig_copies[:2]:
         copy.start()
+    run(TAIL + 1)
     norms[0, 0:1, :] = gain_one + gain_two
     norms[0, 1:2, :] = shift_one + shift_two
     norms[0, 4:8, :] = jnp.zeros((4, width), F32)
     norm_copy(0).start()
     run(TAIL + 2)
-    ng_ref[...] = norms[10]
-    for copy in ig_copies:
+    last_copies = [links.fetch("y", norms.at[10], ng_hbm), links.fetch("z", qg_ref, qg_hbm)]
+    for copy in last_copies:
+        copy.start()
+    for tile in range(tiles):
+        for copy in unit_results(tile):
+            copy.wait()
+    links.fetch("p", pgt_ref, pgt_hbm).wait()
+    for copy in last_copies + ig_copies:
         copy.wait()
 
 
 def collect_kernel(*refs):
-    count = (len(refs) - 3) // 3
+    count = (len(refs) - 5) // 3
     sources, norms, targets = refs[:count], refs[count], refs[count + 1 : 2 * count + 1]
-    target, held, sems = refs[2 * count + 1], refs[2 * count + 2 : 3 * count + 2], refs[-1]
-    loads = [pltpu.make_async_copy(a, b, sems.at[0, n]) for n, (a, b) in enumerate(zip(sources, held))]
-    stores = [pltpu.make_async_copy(a, b, sems.at[1, n]) for n, (a, b) in enumerate(zip(held, targets))]
+    target, held = refs[2 * count + 1], refs[2 * count + 2 : 3 * count + 2]
+    norms_held, target_held, sems = refs[3 * count + 2 :]
+    loads, stores = [], []
+    for source, between, end in zip(sources, held, targets):
+        parts = 4 if source.shape[0] % 64 == 0 else 1
+        size = source.shape[0] // parts
+        for part in range(parts):
+            rows, n = pl.ds(part * size, size), len(loads)
+            loads.append(pltpu.make_async_copy(source.at[rows], between.at[rows], sems.at[0, n]))
+            stores.append(pltpu.make_async_copy(between.at[rows], end.at[rows], sems.at[1, n]))
+    load_norms = pltpu.make_async_copy(norms, norms_held, sems.at[0, len(loads)])
+    store_norms = pltpu.make_async_copy(target_held, target, sems.at[1, len(loads)])
+    load_norms.start()
     for load in loads:
         load.start()
     rows, share = target.shape
     width = norms.shape[1]
     place = lax.broadcasted_iota(jnp.int32, (width, share), 0) - share * lax.axis_index("dp")
     pick = jnp.where(place == lax.broadcasted_iota(jnp.int32, (width, share), 1), 1.0, 0.0)
-    target[...] = lax.dot_general(
-        norms[...], pick, (((1,), (0,)), ((), ())), precision=lax.Precision.HIGHEST, preferred_element_type=F32
+    load_norms.wait()
+    target_held[...] = lax.dot_general(
+        norms_held[...], pick, (((1,), (0,)), ((), ())), precision=lax.Precision.HIGHEST, preferred_element_type=F32
     )[:rows]
+    store_norms.start()
     for load, store in zip(loads, stores):
         load.wait()
         store.start()
-    for store in stores:
+    for store in stores + [store_norms]:
         store.wait()
 
 
@@ -758,11 +799,10 @@
     block, unit, group, tiles = width // 16, 2 * TILE, 3 * UNROLL * HD, hidden // TILE
     heads = heads_width // HD
     S, V = jax.ShapeDtypeStruct, pltpu.VMEM
-    place = pl.BlockSpec(memory_space=pltpu.VMEM)
     far = pl.BlockSpec(memory_space=pl.ANY)
     halves = [2, 2, 2, 2]
     landings = [V((2 * tiles, *halves[1:], block, unit), BF16)]
-    kinds = [(u // 2, u % 2 == 0, unit, False) for u in range(2 * tiles)]
+    kinds = [(u // 2, feed_half(u) == 0, unit, False) for u in range(2 * tiles)]
     kinds += [(tiles, half == 0, heads_width, True) for half in range(2)]
     kinds += [(tiles + 1 + g % 2, g >= 2, group, True) for g in range(4)]
     for pair, keeps, wide, whole in kinds:
@@ -781,9 +821,13 @@
             S((8, width), F32),
         ),
         in_specs=[far] * 11,
-        out_specs=[far, far] + [place] * 5,
+        out_specs=[far] * 7,
         scratch_shapes=[
             pltpu.SemaphoreType.DMA((SEMAPHORES,)),
+            V((3, block, heads_width), F32),
+            V((block, heads_width), F32),
+            V((block, hidden), F32),
+            V((block, hidden), F32),
             V((2, 3, 4, 2, width // 8, heads_width), BF16),
             V((2, 4, 2, heads_width // 8, width), BF16),
             V((2, 4, 2, width // 8, hidden), BF16),
@@ -795,7 +839,8 @@
             V((rows, width), BF16),
             V((width, WIN), BF16),
             V((2, 3, heads_width, WIN), BF16),
-            V((2 * heads, HD, WIN), BF16),
+            V((2 * heads, HD, MID), BF16),
+            V((2 * heads, 1, WIN), F32),
             V((2 * heads, 1, WIN), F32),
             V((heads, 1, rows), F32),
             V((WIN, WIN), F32),
@@ -842,9 +887,10 @@
     out, ig, qg, pgt, ug, dgt, ng = pl.pallas_call(
         collect_kernel,
         out_shape=tuple(S(a.shape, a.dtype) for a in results) + (S((4, share), F32),),
-        in_specs=[far] * 6 + [place],
-        out_specs=[far] * 6 + [place],
-        scratch_shapes=[V(a.shape, a.dtype) for a in results] + [pltpu.SemaphoreType.DMA((2, 6))],
+        in_specs=[far] * 7,
+        out_specs=[far] * 7,
+        scratch_shapes=[V(a.shape, a.dtype) for a in results]
+        + [V(ng.shape, F32), V((4, share), F32), pltpu.SemaphoreType.DMA((2, 24))],
         name="collect",
     )(*results, ng)
     return out, ig, qg.transpose(1, 0, 2), pgt.T, ug, dgt.T, ng

time: 135 us -> 131 us (0.970)
  Pallas kernels: 134 us -> 130 us
    pallas_call x1, Pallas kernels: 129 us -> 127 us  [local(): pl.pallas_call(functools.partial(layer_kernel, dp), out_shape=(S((rows, w...]
where the time goes in v3:
time: 131 us
  Pallas kernels  130 us (99%)
    pallas_call x1, Pallas kernels, local(): pl.pallas_call(functools.partial(layer_kernel, dp), out_shape=(S((rows, w...  127 us
    pallas_call x1, Pallas kernels, local(): pl.pallas_call(collect_kernel, out_shape=tuple((S(a.shape, a.dtype) for a...  3.72 us

profile of v3, /device:TPU:0, one launch (start us, length us, event | category | flops | bytes accessed | tf_op | source)
XLA Modules:
  0.0 131.3 jit_solution(4545290080122394170)
XLA Ops:
  0.6 126.7 %layer.1 = (bf16[1024,768]{1,0:T(8,128)(2,1)}, bf16[1024,768]{1,0:T(8,128)(2,1)}, f32[3,48,384]{2,1,0:T(8,128)}, f32[48,384]{1,0:T(8,128)}, f32[48,1536]{1,0:T(8...) custom-call(bf16[1024,768]{1,0:T(8,128)(2,1)} %x_hbm.1, bf16[1024,768]{1,0:T(8,128)(2,1)} %c_hbm.1, s32[8,128]{1,0:T(8,128)} %bitcast.14, ...), custom_call_target="tpu_custom_call" | custom-call | tf_op jit(solution)/shard_map/layer/pallas_call | solution.py:812
  127.3 3.7 %collect.1 = (bf16[1024,768]{1,0:T(8,128)(2,1)}, bf16[1024,768]{1,0:T(8,128)(2,1)}, f32[3,48,384]{2,1,0:T(8,128)}, f32[48,384]{1,0:T(8,128)}, f32[48,1536]{1,0:T...) custom-call(bf16[1024,768]{1,0:T(8,128)(2,1)} %get-tuple-element.21.refs_0_, bf16[1024,768]{1,0:T(8,128)(2,1)} %get-tuple-element.22.refs_1_, ...), custom_call_target="tpu_custom_call" | custom-call | tf_op jit(solution)/shard_map/collect/pallas_call | solution.py:887

commit v4 on v3

--- a/solution.py
+++ b/solution.py
@@ -78,12 +78,12 @@
     tail = poly * t * bell
     return jnp.where(u >= 0, 1.0 - tail, tail), bell * INV_SQRT_2PI
 ORDERS = (
-    (Y, Z, X, ZZ),
+    (Y, X, Z, ZZ),
     (X, Z, Y, ZZ),
     (Z, X, Y, ZZ),
-    (X, ZZ, Z, Y),
+    (X, Z, ZZ, Y),
     (X, Y, Z, ZZ),
-    (X, Y, Z, ZZ),
+    (X, Z, ZZ, Y),
 )
 SEQUENCE = (0, 1, 2, 3)
 
@@ -110,29 +110,29 @@
     FEED + 2: ((UNIT, 1), (CROSS, UP + 2)),
     MIDWAY + 3: ((CROSS, DOWN + 2),),
     FEED + 3: ((UNIT, 2), (DEEP, QKV)),
-    NEED + 4: ((NEAR, UP + 2), (NEAR, DOWN + 2)),
     FEED + 4: ((UNIT, 3),),
+    NEED + 5: ((NEAR, UP + 2), (NEAR, DOWN + 2)),
     FEED + 5: ((UNIT, 4), (CROSS, QKV)),
     SECOND_NORM: ((UNIT, 5), (UNIT, 2)),
-    SECOND_NORM + 2: ((UNIT, OUT_BLOCKS), (UNIT, 0), (UNIT, OUT_BLOCKS + 1), (UNIT, 4), (UNIT, 3)),
+    SECOND_NORM + 2: ((UNIT, OUT_BLOCKS), (UNIT, OUT_BLOCKS + 1)),
     OTHER: ((NEAR, QKV),),
-    BACK + 0: ((UNIT, OUT_BLOCKS), (UNIT, 5), (UNIT, OUT_BLOCKS + 1)),
-    BACK + 1: ((UNIT, 2), (UNIT, QKV_BLOCKS), (UNIT, 4)),
-    BACK + 2: ((UNIT, 5), (UNIT, QKV_BLOCKS + 1), (UNIT, 0), (UNIT, QKV_BLOCKS)),
-    BACK + 3: ((UNIT, 3), (UNIT, 3), (UNIT, QKV_BLOCKS + 2), (UNIT, 5), (UNIT, OUT_BLOCKS), (UNIT, QKV_BLOCKS + 1)),
-    TAIL: ((UNIT, OUT_BLOCKS + 1), (UNIT, QKV_BLOCKS + 3)),
-    TAIL + 1: ((UNIT, 0), (UNIT, 3)),
+    BACK + 0: ((UNIT, 4), (UNIT, 3), (UNIT, OUT_BLOCKS), (UNIT, 0), (UNIT, OUT_BLOCKS + 1)),
+    BACK + 1: ((UNIT, 5), (UNIT, QKV_BLOCKS), (UNIT, 4), (UNIT, 2)),
+    BACK + 2: ((UNIT, QKV_BLOCKS + 1), (UNIT, 3), (UNIT, OUT_BLOCKS), (UNIT, OUT_BLOCKS + 1), (UNIT, 0)),
+    BACK + 3: ((UNIT, QKV_BLOCKS + 2), (UNIT, OUT_BLOCKS), (UNIT, 5), (UNIT, OUT_BLOCKS + 1)),
+    TAIL: ((UNIT, 3), (UNIT, 0), (UNIT, QKV_BLOCKS), (UNIT, QKV_BLOCKS + 3)),
+    TAIL + 1: ((UNIT, 4), (UNIT, OUT_BLOCKS)),
     TAIL + 2: (
-        (NORM, 0), (UNIT, QKV_BLOCKS + 2), (UNIT, QKV_BLOCKS + 2), (UNIT, 5), (UNIT, OUT_BLOCKS),
-        (UNIT, OUT_BLOCKS + 1), (UNIT, QKV_BLOCKS + 3), (UNIT, QKV_BLOCKS + 3), (NORM, 0), (MERGE, 1), (UNIT, 0),
-        (UNIT, QKV_BLOCKS + 2), (UNIT, QKV_BLOCKS + 3), (NORM, 0), (UNIT, QKV_BLOCKS + 2), (UNIT, QKV_BLOCKS + 3),
-        (NORM, 0), (UNIT, OUT_BLOCKS), (NORM, 0),
+        (UNIT, QKV_BLOCKS + 1), (NORM, 0), (UNIT, 3), (UNIT, QKV_BLOCKS + 2), (UNIT, 0), (MERGE, 1),
+        (UNIT, QKV_BLOCKS + 3), (UNIT, 4), (NORM, 0), (UNIT, QKV_BLOCKS + 2), (UNIT, QKV_BLOCKS + 1),
+        (UNIT, QKV_BLOCKS + 3), (NORM, 0), (UNIT, QKV_BLOCKS + 2), (UNIT, QKV_BLOCKS + 1), (UNIT, QKV_BLOCKS + 3),
+        (NORM, 0), (UNIT, QKV_BLOCKS + 2), (UNIT, QKV_BLOCKS + 3), (NORM, 0),
     ),
 }
 
 
 def feed_half(u):
-    return (u + u // 2 - u // 4) % 2
+    return (u + 1) // 2 % 2
 
 
 def half_index(index, bit):
@@ -238,7 +238,8 @@
             self.first.wait()
             self.held[0][...] += self.kept()
         elif axis == Y:
-            self.meeting.wait()
+            for copy in self.meeting:
+                copy.wait()
             here, there = self.held[self.rank], self.arrival
         else:
             self.copy(axis, self.rank).wait()
@@ -256,12 +257,17 @@
         if axis != Y:
             self.copy(axis, self.rank).start()
         elif self.arrival is None:
-            self.meeting.start()
+            self.meeting[0].start()
 
 
 def pair_up(links, name, keeps, gives):
     rank = keeps.order.index(Y)
-    meeting = links.send((UNIT, name, Y), 0, gives.held[rank], keeps.arrival)
+    source, target = gives.held[rank], keeps.arrival
+    if rank == 0 and name == 0:
+        parts = [(source.at[n], target.at[n]) for n in range(2)]
+    else:
+        parts = [(source, target)]
+    meeting = [links.send((UNIT, name, Y), 0, *part, number=n, many=2) for n, part in enumerate(parts)]
     keeps.meeting = gives.meeting = meeting
 
 
@@ -600,7 +606,7 @@
         links.send("r", 0, fed, out_hbm.at[feed_rows]),
         links.fetch("s", fed, out_hbm.at[feed_rows]),
     ]
-    for copy in edge_copies + out_copies:
+    for copy in edge_copies + blocks[0].meeting[1:] + out_copies:
         copy.start()
     run(SECOND_NORM)
     ct[...] = cw[...].T

time: 131 us -> 132 us (level)
  no operation moved by 1% of the time
where the time goes in v4:
time: 132 us
  Pallas kernels  131 us (99%)
    pallas_call x1, Pallas kernels, local(): pl.pallas_call(functools.partial(layer_kernel, dp), out_shape=(S((rows, w...  127 us
    pallas_call x1, Pallas kernels, local(): pl.pallas_call(collect_kernel, out_shape=tuple((S(a.shape, a.dtype) for a...  3.72 us

profile of v4, /device:TPU:0, one launch (start us, length us, event | category | flops | bytes accessed | tf_op | source)
XLA Modules:
  0.0 131.7 jit_solution(1599471408683262856)
XLA Ops:
  0.6 127.1 %layer.1 = (bf16[1024,768]{1,0:T(8,128)(2,1)}, bf16[1024,768]{1,0:T(8,128)(2,1)}, f32[3,48,384]{2,1,0:T(8,128)}, f32[48,384]{1,0:T(8,128)}, f32[48,1536]{1,0:T(8...) custom-call(bf16[1024,768]{1,0:T(8,128)(2,1)} %x_hbm.1, bf16[1024,768]{1,0:T(8,128)(2,1)} %c_hbm.1, s32[8,128]{1,0:T(8,128)} %bitcast.14, ...), custom_call_target="tpu_custom_call" | custom-call | tf_op jit(solution)/shard_map/layer/pallas_call | solution.py:818
  127.7 3.7 %collect.1 = (bf16[1024,768]{1,0:T(8,128)(2,1)}, bf16[1024,768]{1,0:T(8,128)(2,1)}, f32[3,48,384]{2,1,0:T(8,128)}, f32[48,384]{1,0:T(8,128)}, f32[48,1536]{1,0:T...) custom-call(bf16[1024,768]{1,0:T(8,128)(2,1)} %get-tuple-element.21.refs_0_, bf16[1024,768]{1,0:T(8,128)(2,1)} %get-tuple-element.22.refs_1_, ...), custom_call_target="tpu_custom_call" | custom-call | tf_op jit(solution)/shard_map/collect/pallas_call | solution.py:893
